TPU v7x, 256 devices: a whole 4x4x8 slice. The times are simulated.
256 devices in a mesh: lon: 16 (over z, x_lo), lat: 8 (over y, core), lev: 2 (over x_hi).
Axes of the slice: x: 4 (x_hi: 2, x_lo: 2; x = x_hi * 2 + x_lo), y: 4, z: 8, core: 2. Of those that a mesh axis runs over, the one named last changes fastest.
Arguments:
- state: float32 [5, 16, 128, 8192], P(None, 'lev', 'lat', 'lon'), may hold values from -6 to 6
- mask: int32 [16, 128, 8192], P('lev', 'lat', 'lon'), may hold values 0 or 1
- coriolis: float32 [128], P('lat'), may hold values from 0.05 to 0.3
- penetration: float32 [16], P('lev'), may hold values from 0.05 to 1
- flux_tiles: float32 [16384, 3, 512], P(('lon', 'lat')), may hold values from -4 to 4
- flux_owner: int32 [16384, 1], P(('lon', 'lat')), may hold values from 0 to 127; in each aligned block of 128 rows (0 to 127, 128 to 255, ...) at most 2 rows name the same one
- flux_row: int32 [16384], P(('lon', 'lat')), may hold values from 0 to 15
- fold_partner: int32 [8192], replicated, may hold values from 0 to 8191, as said below
Outputs:
- new_state: float32 [5, 16, 128, 8192], P(None, 'lev', 'lat', 'lon')
Inputs may be any that keep to these rules, and one draw needn't show every extreme that they name: `flux_owner`: among the 128 tiles of one device at most 2 name the same owner, and some owner receives exactly 2 from some device. fold_partner[i] = (h - i) mod 8192 for one hinge column h.
All inputs are finite; a program needn't handle non-finite values. No bound on the sum of `mask` on one device may be relied on, other than what follows from the above.
Results may differ from a plain program's by a relative error of at most 0.0003.
Values sent between devices are 32-bit elements; how exact they have to be, the bound alone decides.
A program may use at most 192 MiB of HBM per device.

v0:
```python
import jax
import jax.numpy as jnp
from jax import lax
from jax.sharding import PartitionSpec as P

STEPS = 2


ALPHA = 0.2
BETA = 0.15
PRESS = 0.1
VISCOUS = 0.1
DIFFUSE = 0.1
ADVECT = 0.1


def padded(value, sides, width, wrap):
    for axis, dim in sides:
        peers, length = (lax.axis_size(axis), value.shape[dim])
        up = [(i, (i + 1) % peers) for i in range(peers if wrap else peers - 1)]
        down = [(j, i) for i, j in up]
        last = lax.slice_in_dim(value, length - width, length, axis=dim)
        initial = lax.slice_in_dim(value, 0, width, axis=dim)
        before = lax.ppermute(last, axis, up)
        after = lax.ppermute(initial, axis, down)
        value = jnp.concatenate([before, value, after], axis=dim)
    return value


def carried_in(value, axis, combine, identity):
    peers, place = (lax.axis_size(axis), lax.axis_index(axis))
    everything = lax.all_gather(value, axis)
    start = jnp.broadcast_to(jnp.asarray(identity, value.dtype), value.shape)

    def hop(k, before):
        reached = k < place
        new = combine(before, everything[k])
        return jnp.where(reached, new, before)

    return lax.fori_loop(0, peers, hop, start)


def receive_flux(flux_tiles, flux_owner, flux_row, rows, cols):
    lat_count = lax.axis_size("lat")
    lon_count = lax.axis_size("lon")
    owners = lat_count * lon_count
    tiles = flux_tiles.shape[0]
    capacity = max(2, 2 * tiles // owners)
    owner = flux_owner[:, 0]
    hits = (owner[:, None] == jnp.arange(owners, dtype=jnp.int32)[None, :]).astype(jnp.int32)
    before = jnp.cumsum(hits, axis=0) - hits
    slot = jnp.sum(before * hits, axis=1)
    target = owner * capacity + slot
    placing = target[None, :] == jnp.arange(owners * capacity, dtype=jnp.int32)[:, None]
    packed = jnp.dot(
        placing.astype(jnp.float32),
        flux_tiles.reshape(tiles, 3 * cols),
        precision=lax.Precision.HIGHEST,
    )
    slot_rows = jnp.sum(placing.astype(jnp.int32) * (flux_row[None, :] + 1), axis=1) - 1
    arrived, arrived_rows = (
        lax.all_to_all(
            packed.reshape(owners, capacity, 3 * cols),
            ("lon", "lat"),
            split_axis=0,
            concat_axis=0,
            tiled=True,
        ),
        lax.all_to_all(
            slot_rows.reshape(owners, capacity),
            ("lon", "lat"),
            split_axis=0,
            concat_axis=0,
            tiled=True,
        ),
    )
    arrived = arrived.reshape(owners * capacity, 3 * cols)
    arrived_rows = arrived_rows.reshape(owners * capacity)
    landing = (arrived_rows[None, :] == jnp.arange(rows, dtype=jnp.int32)[:, None]).astype(
        jnp.float32
    )
    summed = jnp.dot(landing, arrived, precision=lax.Precision.HIGHEST)
    return summed.reshape(rows, 3, cols).transpose(1, 0, 2)


def advance(state, wet, turning, absorb, forcing, partner):
    fields, levels, rows, cols = state.shape
    lat_count = lax.axis_size("lat")
    lat_place = lax.axis_index("lat")
    signs = jnp.array([-1.0, -1.0, 1.0, 1.0, 1.0], jnp.float32)
    lon_ext = padded(state, (("lon", 3),), 1, True)
    lat_ext = padded(state, (("lat", 2),), 1, False)
    whole_top = lax.all_gather(state[:, :, rows - 1, :], "lon", axis=2, tiled=True)
    mirrored = jnp.take(whole_top, partner, axis=2) * signs[:, None, None]
    north_edge = jnp.where(lat_place == lat_count - 1, mirrored, lat_ext[:, :, rows + 1, :])
    south_edge = jnp.where(lat_place == 0, state[:, :, 0, :], lat_ext[:, :, 0, :])
    east_all = lon_ext[:, :, :, 2:]
    west_all = lon_ext[:, :, :, :-2]
    north_all = jnp.concatenate([lat_ext[:, :, 2 : rows + 1, :], north_edge[:, :, None, :]], axis=2)
    south_all = jnp.concatenate([south_edge[:, :, None, :], lat_ext[:, :, 1:rows, :]], axis=2)
    sets = jnp.stack([state, east_all, west_all, north_all, south_all])
    buoyancy = ALPHA * sets[:, 2] - BETA * sets[:, 3]
    running = jnp.cumsum(buoyancy, axis=1)
    column_total = running[:, -1]
    prefix = carried_in(
        column_total, "lev", lambda earlier, later: earlier + later, jnp.zeros_like(column_total)
    )
    pressure = PRESS * (prefix[:, None] + running - 0.5 * buoyancy)
    slope_x = 0.5 * (pressure[1] - pressure[2])
    slope_y = 0.5 * (pressure[3] - pressure[4])
    zonal, merid = (state[0], state[1])
    result = []
    for field in range(5):
        value = state[field]
        east = east_all[field]
        west = west_all[field]
        north = north_all[field]
        south = south_all[field]
        laplace = east + west + north + south - 4.0 * value
        if field == 0:
            trend = turning * merid - slope_x + VISCOUS * laplace
        elif field == 1:
            trend = -turning * zonal - slope_y + VISCOUS * laplace
        else:
            trend = (
                DIFFUSE * laplace
                - ADVECT * (zonal * (0.5 * (east - west)) + merid * (0.5 * (north - south)))
                + absorb * forcing[field - 2][None]
            )
        result.append(value + wet * trend)
    return jnp.stack(result)


def body(state, mask, coriolis, penetration, flux_tiles, flux_owner, flux_row, fold_partner):
    fields, levels, rows, cols = state.shape
    forcing = receive_flux(flux_tiles, flux_owner, flux_row, rows, cols)
    partner = lax.dynamic_slice_in_dim(fold_partner, lax.axis_index("lon") * cols, cols)
    wet = mask.astype(jnp.float32)
    turning = coriolis[None, :, None]
    absorb = penetration[:, None, None]
    for substep in range(STEPS):
        state = advance(state, wet, turning, absorb, forcing, partner)
    return state


def solution(mesh):
    return jax.shard_map(
        body,
        mesh=mesh,
        in_specs=(
            P(None, "lev", "lat", "lon"),
            P("lev", "lat", "lon"),
            P("lat"),
            P("lev"),
            P(("lon", "lat"), None, None),
            P(("lon", "lat"), None),
            P(("lon", "lat")),
            P(),
        ),
        out_specs=P(None, "lev", "lat", "lon"),
        check_vma=False,
    )
```

profile of v0, /device:TPU:4, one launch (start us, length us, event | category | flops | bytes accessed | tf_op | source)
XLA Modules:
  0.0 294.1 jit_solution(14907617382182979369)
XLA Ops:
  6.5 1.5 fusion.204
  8.1 2.4 collective-permute-start.3
  10.5 2.0 fusion.202
  12.5 1.2 collective-permute-start.1
  13.7 5.3 %collective-permute-start = (f32[5,8,16,1]{3,2,1,0:T(8,128)}, f32[5,8,16,1]{3,2,1,0:T(8,128)}, u32[]{:S(2)}, u32[]{:S(2)}) collective-permute-start(f32[5,8,16,1]{3,2,1,0:T(8,128)} %get-tuple-element.230), channel_id=1, source_target_pairs={{16,0},{32,16},{48,32},{64,48},{80,64},{96,80},{112,96},{128,112},... | collective-permute-start | bytes 7688 | tf_op jit(solution)/shard_map/ppermute | solution.py:25
  20.4 11.5 %all-to-all-start = ((s32[128,1,2]{2,1,0:T(1,128)}), s32[128,1,2]{2,1,0:T(1,128)}, u32[]{:S(2)}, u32[]{:S(2)}) async-start(s32[128,1,2]{2,1,0:T(1,128)} %bitcast.25), calls=%async_computation | async-start | bytes 131072 | tf_op jit(solution)/shard_map/all_to_all | solution.py:69
  32.9 1.2 constant_dynamic-update-slice_fusion.1
  34.1 2.1 fusion.182
  36.2 1.3 bitcast_dynamic-update-slice_fusion.1
  37.5 1.3 fusion.203
  39.4 3.8 %copy.139 = f32[128,2,1536]{2,1,0:T(2,128)} copy(f32[128,2,1536]{2,0,1:T(8,128)} %fusion.182) | data formatting | bytes 3145728 | tf_op jit(solution)/shard_map/dot_general | solution.py:55
  43.2 12.6 %all-to-all-start.1 = ((f32[128,2,1536]{2,1,0:T(2,128)}), f32[128,2,1536]{2,1,0:T(2,128)}, u32[]{:S(2)}, u32[]{:S(2)}) async-start(f32[128,2,1536]{2,1,0:T(2,128)} %copy.139), calls=%async_computation.1 | async-start | bytes 3145728 | tf_op jit(solution)/shard_map/all_to_all | solution.py:62
  56.5 1.7 reduce.3
  58.3 1.8 constant_dynamic-update-slice_fusion
  60.1 2.9 fusion.27
  63.0 1.5 collective-permute-start.2
  64.5 1.5 fusion.10
  66.2 2.0 copy.131
  68.2 24.8 %all-gather.7.cloned.1.call-done = f32[5,8,1,8192]{3,1,2,0:T(8,128)} async-done(((f32[5,8,1,512]{3,1,2,0:T(8,128)}), f32[5,8,1,8192]{3,1,2,0:T(8,128)}) %all-gather.7.cloned.1.call-update) | async-done | bytes 1310736 | tf_op jit(solution)/shard_map/all_gather | solution.py:93
  92.9 16.6 %copy.129 = f32[5,8,1,8192]{1,0,3,2:T(8,128)} copy(f32[5,8,1,8192]{3,1,2,0:T(8,128)} %all-gather.7.cloned.1.call-done) | data formatting | bytes 2621440 | tf_op jit(solution)/shard_map/all_gather | solution.py:93
  109.5 4.8 %gather_fusion = f32[512,5,8]{2,1,0:T(8,128)} fusion(f32[5,8,8192]{1,0,2:T(8,128)} %bitcast.490, s32[1024]{0:T(1024)S(1)} %pad_clamp_fusion), kind=kCustom, calls=%fused_computation.clone | custom fusion | bytes 165888 | tf_op jit(solution)/shard_map/jit(_take)/gather | solution.py:94
  114.3 4.2 %fusion.1 = f32[5,8,1,512]{1,0,3,2:T(8,128)} fusion(f32[5,8,1,512]{1,0,3,2:T(8,128)} %copy.131, f32[512,5,8]{2,1,0:T(8,128)} %gather_fusion, f32[5]{0:T(128)S(1)} %copy-done.34, pred[512]{0:T(512)(128)(4,1)S(1)} %get-tuple-element.222, pred[]{:T(512)S(6)} %eq.66), kind=kLoop, calls=%fused_computation.47 | loop fusion | flops 61440 | bytes 246293 | tf_op jit(solution)/shard_map/broadcast_in_dim | solution.py:99
  118.5 2.0 copy.132
  120.4 1.3 fusion.18
  122.2 1.3 fusion.16
  123.5 2.0 fusion.28
  125.5 7.6 %all-gather.1 = f32[10,1,16,512]{3,2,1,0:T(8,128)} all-gather(f32[5,1,16,512]{3,2,1,0:T(8,128)S(1)} %slice.354), channel_id=3, replica_groups=mesh['lon'=16,'lat'=8,'lev'=2] {'lev'}, dimensions={0}, use_global_device_ids=true | all-gather | bytes 491520 | tf_op jit(solution)/shard_map/all_gather | solution.py:32
  133.2 2.0 while.28
  134.2 1.0 add_select_fusion.4
  135.2 2.4 subtract_multiply_fusion.1
  137.7 2.0 bitcast_dynamic-update-slice_fusion.6
  139.7 2.0 bitcast_dynamic-update-slice_fusion.5
  141.7 3.2 %reshape.127 = f32[256,1536]{1,0:T(8,128)} reshape(f32[128,2,1536]{2,1,0:T(2,128)} %all-to-all-done.1) | data formatting | bytes 3145728 | tf_op jit(solution)/shard_map/reshape | solution.py:77
  144.9 3.1 %copy.140 = f32[1536,256]{1,0:T(8,128)} copy(f32[1536,256]{0,1:T(8,128)} %bitcast.492) | data formatting | bytes 3145728 | tf_op jit(solution)/shard_map/dot_general | solution.py:82
  148.0 2.3 convolution_bitcast_fusion
  150.4 2.2 bitcast_dynamic-update-slice_fusion.4
  152.6 2.0 bitcast_dynamic-update-slice_fusion.3
  154.6 2.0 bitcast_dynamic-update-slice_fusion.2
  158.0 1.3 collective-permute-start.7
  159.5 2.4 collective-permute-start.4
  161.9 1.3 fusion.201
  163.2 1.2 bitcast_dynamic-update-slice_fusion
  164.5 6.3 %collective-permute-done.4 = f32[5,8,16,1]{3,2,1,0:T(8,128)S(1)} collective-permute-done((f32[5,8,16,1]{3,2,1,0:T(8,128)S(1)}, f32[5,8,16,1]{3,2,1,0:T(8,128)S(1)}, u32[]{:S(2)}, u32[]{:S(2)}) %collective-permute-start.4) | collective-permute-done | bytes 2592 | tf_op jit(solution)/shard_map/ppermute | solution.py:25
  170.7 1.5 fusion.7
  172.3 1.5 collective-permute-start.6
  173.8 4.0 %collective-permute-done.5 = f32[5,8,16,1]{3,2,1,0:T(8,128)S(1)} collective-permute-done((f32[5,8,16,1]{3,2,1,0:T(8,128)S(1)}, f32[5,8,16,1]{3,2,1,0:T(8,128)S(1)}, u32[]{:S(2)}, u32[]{:S(2)}) %collective-permute-start.5) | collective-permute-done | bytes 2592 | tf_op jit(solution)/shard_map/ppermute | solution.py:24
  177.8 1.5 fusion.4
  180.0 2.9 copy.144
  182.9 50.8 %all-gather.9.cloned.1.call-done = f32[5,8,1,8192]{3,1,2,0:T(8,128)} async-done(((f32[5,8,1,512]{3,1,2,0:T(8,128)}), f32[5,8,1,8192]{3,1,2,0:T(8,128)}) %all-gather.9.cloned.1.call-update) | async-done | bytes 1310736 | tf_op jit(solution)/shard_map/all_gather | solution.py:93
  233.7 16.6 %copy.142 = f32[5,8,1,8192]{1,0,3,2:T(8,128)} copy(f32[5,8,1,8192]{3,1,2,0:T(8,128)} %all-gather.9.cloned.1.call-done) | data formatting | bytes 2621440 | tf_op jit(solution)/shard_map/all_gather | solution.py:93
  250.3 4.8 %gather_fusion.1 = f32[512,5,8]{2,1,0:T(8,128)} fusion(f32[5,8,8192]{1,0,2:T(8,128)} %bitcast.489, s32[1024]{0:T(1024)S(1)} %pad_clamp_fusion), kind=kCustom, calls=%fused_computation.1.clone | custom fusion | bytes 165888 | tf_op jit(solution)/shard_map/jit(_take)/gather | solution.py:94
  255.1 4.2 %fusion = f32[5,8,1,512]{1,0,3,2:T(8,128)} fusion(f32[5,8,1,512]{1,0,3,2:T(8,128)} %copy.144, f32[512,5,8]{2,1,0:T(8,128)} %gather_fusion.1, f32[5]{0:T(128)S(1)} %copy-done.35, pred[512]{0:T(512)(128)(4,1)S(1)} %get-tuple-element.222, pred[]{:T(512)S(6)} %eq.66), kind=kLoop, calls=%fused_computation.44 | loop fusion | flops 61440 | bytes 246293 | tf_op jit(solution)/shard_map/broadcast_in_dim | solution.py:99
  259.3 2.6 copy.145
  261.9 2.2 fusion.14
  264.1 1.3 fusion.12
  265.4 2.0 fusion.30
  267.4 1.1 copy-done.12
  268.5 7.6 %all-gather.3 = f32[10,1,16,512]{3,2,1,0:T(8,128)} all-gather(f32[5,1,16,512]{3,2,1,0:T(8,128)S(1)} %slice.407), channel_id=5, replica_groups=mesh['lon'=16,'lat'=8,'lev'=2] {'lev'}, dimensions={0}, use_global_device_ids=true | all-gather | bytes 491520 | tf_op jit(solution)/shard_map/all_gather | solution.py:32
  276.1 3.3 %while.29 = (s32[]{:T(128)}, f32[5,16,512]{2,1,0:T(8,128)}, s32[]{:T(128)}, f32[2,5,16,512]{3,2,1,0:T(8,128)}, s32[]{:T(128)}, /*index=5*/s32[]{:T(128)}) while((s32[]{:T(128)}, f32[5,16,512]{2,1,0:T(8,128)}, s32[]{:T(128)}, f32[2,5,16,512]{3,2,1,0:T(8,128)}, s32[]{:T(128)}, /*index=5*/s32[]{:T(128)}) %tuple.87), condition=%wide.region_8.10_spmd.clone, body=%wide.region_7.9_spmd.clone.sunk | while | flops 122884 | bytes 491621 | solution.py:40
  276.1 1.6 add_select_fusion.5
  277.7 1.7 add_select_fusion.5
  279.4 2.8 subtract_multiply_fusion
  285.2 1.0 copy-done.28
  286.2 1.1 fusion.49
  (121 shorter events, 10.9 us)
Async XLA Ops:
  6.5 12.5 %copy-start.30 = (s32[128,1]{0,1:T(1,128)S(1)}, s32[128,1]{0,1:T(1,128)}, u32[]{:S(2)}) copy-start(s32[128,1]{0,1:T(1,128)} %param.21) | copy-start | bytes 1540
  6.5 12.9 %copy-start.38 = (s32[128]{0:T(128)S(1)}, s32[128]{0:T(128)}, u32[]{:S(2)}) copy-start(s32[128]{0:T(128)} %param.22) | copy-start | bytes 1540
  6.5 25.3 %copy-start.19 = (f32[128,3,512]{2,0,1:T(8,128)S(1)}, f32[128,3,512]{2,0,1:T(8,128)}, u32[]{:S(2)}) copy-start(f32[128,3,512]{2,0,1:T(8,128)} %param.20) | copy-start | bytes 2359300
  6.5 86.4 %all-gather.7.cloned.1.call-start = ((), (), s32[]{:S(2)}) async-start(), calls=%async_computation.2 | async-start | bytes 1392640 | tf_op jit(solution)/shard_map/all_gather | solution.py:93
  8.1 2.4 copy-start.21
  8.1 54.9 %collective-permute-start.3 = (f32[5,8,1,512]{3,1,2,0:T(8,128)S(1)}, f32[5,8,1,512]{3,1,2,0:T(8,128)}, u32[]{:S(2)}, u32[]{:S(2)}) collective-permute-start(f32[5,8,1,512]{3,1,2,0:T(8,128)S(1)} %copy.151), channel_id=1, source_target_pairs={{0,2},{2,4},{4,6},{6,8},{8,10},{10,12},{12,14},{1,3},{3,5},{5,7},{... | collective-permute-start | bytes 245768 | tf_op jit(solution)/shard_map/ppermute | solution.py:24
  12.5 20.4 %copy-start = (f32[5,8,16,512]{3,2,1,0:T(8,128)S(1)}, f32[5,8,16,512]{3,2,1,0:T(8,128)}, u32[]{:S(2)}) copy-start(f32[5,8,16,512]{3,2,1,0:T(8,128)} %param.16) | copy-start | bytes 3932164
  12.5 52.0 %collective-permute-start.1 = (f32[5,8,16,1]{3,2,1,0:T(8,128)}, f32[5,8,16,1]{3,2,1,0:T(8,128)S(1)}, u32[]{:S(2)}, u32[]{:S(2)}) collective-permute-start(f32[5,8,16,1]{3,2,1,0:T(8,128)} %get-tuple-element.231), channel_id=1, source_target_pairs={{0,16},{16,32},{32,48},{48,64},{64,80},{80,96},{96,112},{112,128},... | collective-permute-start | bytes 7688 | tf_op jit(solution)/shard_map/ppermute | solution.py:24
  13.7 44.6 %collective-permute-start = (f32[5,8,16,1]{3,2,1,0:T(8,128)}, f32[5,8,16,1]{3,2,1,0:T(8,128)}, u32[]{:S(2)}, u32[]{:S(2)}) collective-permute-start(f32[5,8,16,1]{3,2,1,0:T(8,128)} %get-tuple-element.230), channel_id=1, source_target_pairs={{16,0},{32,16},{48,32},{64,48},{80,64},{96,80},{112,96},{128,112},... | collective-permute-start | bytes 7688 | tf_op jit(solution)/shard_map/ppermute | solution.py:25
  20.4 22.8 %all-to-all-start = ((s32[128,1,2]{2,1,0:T(1,128)}), s32[128,1,2]{2,1,0:T(1,128)}, u32[]{:S(2)}, u32[]{:S(2)}) async-start(s32[128,1,2]{2,1,0:T(1,128)} %bitcast.25), calls=%async_computation | async-start | bytes 131072 | tf_op jit(solution)/shard_map/all_to_all | solution.py:69
  37.5 1.3 copy-start.31
  38.8 81.7 %copy-start.1 = (f32[5,8,15,512]{3,2,1,0:T(8,128)}, f32[5,8,15,512]{3,2,1,0:T(8,128)S(1)}, u32[]{:S(2)}) copy-start(f32[5,8,15,512]{3,2,1,0:T(8,128)S(1)} %get-tuple-element.232) | copy-start | bytes 3686404
  43.2 98.5 %all-to-all-start.1 = ((f32[128,2,1536]{2,1,0:T(2,128)}), f32[128,2,1536]{2,1,0:T(2,128)}, u32[]{:S(2)}, u32[]{:S(2)}) async-start(f32[128,2,1536]{2,1,0:T(2,128)} %copy.139), calls=%async_computation.1 | async-start | bytes 3145728 | tf_op jit(solution)/shard_map/all_to_all | solution.py:62
  55.8 177.9 %all-gather.9.cloned.1.call-start = ((), (), s32[]{:S(2)}) async-start(), calls=%async_computation.3 | async-start | bytes 1392640 | tf_op jit(solution)/shard_map/all_gather | solution.py:93
  63.0 3.2 %collective-permute-start.2 = (f32[5,8,1,512]{3,1,2,0:T(8,128)S(1)}, f32[5,8,1,512]{3,1,2,0:T(8,128)S(1)}, u32[]{:S(2)}, u32[]{:S(2)}) collective-permute-start(f32[5,8,1,512]{3,1,2,0:T(8,128)S(1)} %get-tuple-element.241), channel_id=1, source_target_pairs={{2,0},{4,2},{6,4},{8,6},{10,8},{12,10},{14,12},{3,1},{5,3},{7,5},{... | collective-permute-start | bytes 245768 | tf_op jit(solution)/shard_map/ppermute | solution.py:25
  68.2 46.2 %copy-start.34 = (f32[5]{0:T(128)S(1)}, f32[5]{0:T(128)}, u32[]{:S(2)}) copy-start(f32[5]{0:T(128)} %constant.108.clone) | copy-start | bytes 64
  120.4 1.8 copy-start.4
  135.1 2.4 copy-start.2
  135.2 2.5 copy-start.5
  135.2 2.5 copy-start.9
  135.2 2.5 copy-start.32
  137.7 2.0 copy-start.36
  148.0 2.4 copy-start.3
  148.0 2.4 copy-start.29
  150.3 2.3 copy-start.26
  150.3 2.3 copy-start.24
  150.3 4.3 %copy-start.22 = (f32[16,512]{1,0:T(8,128)}, f32[16,512]{1,0:T(8,128)S(1)}, u32[]{:S(2)}) copy-start(f32[16,512]{1,0:T(8,128)S(1)} %get-tuple-element.236) | copy-start | bytes 98308
  150.4 2.2 copy-start.6
  158.0 14.2 %collective-permute-start.7 = (f32[5,8,1,512]{3,1,2,0:T(8,128)}, f32[5,8,1,512]{3,1,2,0:T(8,128)S(1)}, u32[]{:S(2)}, u32[]{:S(2)}) collective-permute-start(f32[5,8,1,512]{3,1,2,0:T(8,128)} %copy.155), channel_id=1, source_target_pairs={{0,2},{2,4},{4,6},{6,8},{8,10},{10,12},{12,14},{1,3},{3,5},{5,7},{... | collective-permute-start | bytes 245768 | tf_op jit(solution)/shard_map/ppermute | solution.py:24
  159.5 11.2 %collective-permute-start.4 = (f32[5,8,16,1]{3,2,1,0:T(8,128)S(1)}, f32[5,8,16,1]{3,2,1,0:T(8,128)S(1)}, u32[]{:S(2)}, u32[]{:S(2)}) collective-permute-start(f32[5,8,16,1]{3,2,1,0:T(8,128)S(1)} %get-tuple-element.226), channel_id=1, source_target_pairs={{16,0},{32,16},{48,32},{64,48},{80,64},{96,80},{112,96},{128,112},... | collective-permute-start | bytes 7688 | tf_op jit(solution)/shard_map/ppermute | solution.py:25
  164.5 7.8 %copy-start.20 = (f32[5,8,1,512]{3,2,1,0:T(1,128)S(1)}, f32[5,8,1,512]{3,2,1,0:T(1,128)}, u32[]{:S(2)}) copy-start(f32[5,8,1,512]{3,2,1,0:T(1,128)} %get-tuple-element.224) | copy-start | bytes 245764
  164.5 13.4 %collective-permute-start.5 = (f32[5,8,16,1]{3,2,1,0:T(8,128)S(1)}, f32[5,8,16,1]{3,2,1,0:T(8,128)S(1)}, u32[]{:S(2)}, u32[]{:S(2)}) collective-permute-start(f32[5,8,16,1]{3,2,1,0:T(8,128)S(1)} %get-tuple-element.227), channel_id=1, source_target_pairs={{0,16},{16,32},{32,48},{48,64},{64,80},{80,96},{96,112},{112,128},... | collective-permute-start | bytes 7688 | tf_op jit(solution)/shard_map/ppermute | solution.py:24
  172.3 7.7 %collective-permute-start.6 = (f32[5,8,1,512]{3,1,2,0:T(8,128)S(1)}, f32[5,8,1,512]{3,1,2,0:T(8,128)}, u32[]{:S(2)}, u32[]{:S(2)}) collective-permute-start(f32[5,8,1,512]{3,1,2,0:T(8,128)S(1)} %get-tuple-element.239), channel_id=1, source_target_pairs={{2,0},{4,2},{6,4},{8,6},{10,8},{12,10},{14,12},{3,1},{5,3},{7,5},{... | collective-permute-start | bytes 245768 | tf_op jit(solution)/shard_map/ppermute | solution.py:25
  182.9 72.2 %copy-start.35 = (f32[5]{0:T(128)S(1)}, f32[5]{0:T(128)}, u32[]{:S(2)}) copy-start(f32[5]{0:T(128)} %constant.108.clone) | copy-start | bytes 64
  261.9 2.3 copy-start.7
  261.9 2.3 copy-start.14
  267.4 1.1 copy-start.12
  279.4 2.8 copy-start.8
  279.4 2.8 copy-start.10
  279.4 2.8 copy-start.11
  279.4 2.9 copy-start.13
  279.4 2.9 copy-start.15
  279.4 2.9 copy-start.33
  282.3 0.6 copy-start.37
  282.9 0.9 copy-start.18
  282.9 1.0 copy-start.27
  283.8 1.0 copy-start.17
  283.8 1.0 copy-start.25
  284.8 1.4 copy-start.16
  284.8 1.4 copy-start.23
  285.1 1.1 copy-start.28
Sparse Core Ops, SparseCore 0:
  10.6 82.2 all-gather.6
  158.2 75.5 all-gather.8
where the time goes:
time: 296 us; the launch traced here: 294 us
  waiting for transfers between devices  86 us (29%)
  local copies, waits for them, and re-layouts  85.2 us (29%)
  other arithmetic  49.6 us (17%)
  starting transfers between devices  39.7 us (13%)
  blocking collectives  15.2 us (5%)
  between operations  13.9 us (5%)
  matrix products  4.37 us (1%)
    all_gather x2, waiting for transfers between devices, advance(): lax.all_gather(state[:, :, rows - 1, :], 'lon', axis=2, tiled=True)  75.6 us
    all_gather x2, local copies, waits for them, and re-layouts, advance(): lax.all_gather(state[:, :, rows - 1, :], 'lon', axis=2, tiled=True)  33.2 us
    unnamed x17, other arithmetic  17.7 us
    all_gather x2, blocking collectives, carried_in(): everything = lax.all_gather(value, axis)  15.2 us
    all_to_all x1, starting transfers between devices, receive_flux(): lax.all_to_all(packed.reshape(owners, capacity, 3 * cols), ('lon', 'lat')...  12.6 us
    unnamed x85, local copies, waits for them, and re-layouts  11.8 us
    all_to_all x1, starting transfers between devices, receive_flux(): lax.all_to_all(slot_rows.reshape(owners, capacity), ('lon', 'lat'), split...  11.5 us
    ppermute x4, starting transfers between devices, padded(): after = lax.ppermute(initial, axis, down)  10.7 us
  transfers between devices with their start and end apart: 12, of which 5 were waited for; matrix products, arithmetic and copies ran while one was open for 25% of the time, Pallas kernels for 0%

commit v1 on v0

v1 whole, which is shorter than its diff:
```python
import functools
import math

import jax
import jax.numpy as jnp
from jax import lax
from jax.experimental import pallas as pl
from jax.experimental.pallas import tpu as pltpu
from jax.sharding import PartitionSpec as P

ALPHA, BETA, PRESS = 0.2, 0.15, 0.1
VISCOUS, DIFFUSE, ADVECT = 0.1, 0.1, 0.1
F32, BF16, I32 = jnp.float32, jnp.bfloat16, jnp.int32
MESH = pl.DeviceIdType.MESH

ROWS, EXT = 16, 24


def split3(x):
    hi = x.astype(BF16)
    rest = x - hi.astype(F32)
    mid = rest.astype(BF16)
    low = (rest - mid.astype(F32)).astype(BF16)
    return hi, mid, low


def iota(shape, dim):
    return lax.broadcasted_iota(I32, shape, dim)


def substep(q, m, prefix, running, turning):
    width = q[0].shape[1]
    east = lambda a: pltpu.roll(a, width - 1, 1)
    west = lambda a: pltpu.roll(a, 1, 1)
    north = lambda a: pltpu.roll(a, EXT - 1, 0)
    south = lambda a: pltpu.roll(a, 1, 0)
    u, v = q[0], q[1]
    b = ALPHA * q[2] - BETA * q[3]
    running = running + b
    p = PRESS * (prefix + running - 0.5 * b)
    px = 0.5 * (east(p) - west(p))
    py = 0.5 * (north(p) - south(p))
    new = []
    for f in range(5):
        e, w, n, s = east(q[f]), west(q[f]), north(q[f]), south(q[f])
        lap = (e + w) + (n + s) - 4.0 * q[f]
        if f == 0:
            trend = turning * v - px + VISCOUS * lap
        elif f == 1:
            trend = VISCOUS * lap - turning * u - py
        else:
            trend = DIFFUSE * lap - (0.5 * ADVECT) * (u * (e - w) + v * (n - s))
        new.append(q[f] + m * trend)
    return new, running


def exchange_kernel(
    nlon, nlat, tiles, nk, W,
    state, mask, cor, pen, flux, owner_ref, row_ref, hinge, fold_lo, fold_hi,
    X, FX, PX,
    tbuf, mbuf, pk, got, meta, metas, dense, zgot, half, partner, frow, rowsgot, colsgot, foldgot,
    hsend, hgot, esend, egot, levs, levg, lev2s, lev2g, cors, mirror,
    ld, ms, mr, ss, sr, zs, zr, hs, hr, es, er, ls, lr, ps, pr, rs, rr, cs, cr, fs, fr,
):
    lon, lat, lev = lax.axis_index("lon"), lax.axis_index("lat"), lax.axis_index("lev")
    nz, NP = nlon // 2, 2 * nlat
    z, xl = lon // 2, lon % 2
    me = xl * nlat + lat
    HW = W // 2
    WX = W + 128
    N = NP * 2 * nz
    nfk = 6 * nk
    other = 1 - lev
    top, bottom = lat == nlat - 1, lat == 0

    def plane(p):
        return {"lon": z * 2 + p // nlat, "lat": p % nlat}

    def remote(src, dst, send, recv, device):
        return pltpu.make_async_remote_copy(
            src_ref=src, dst_ref=dst, send_sem=send, recv_sem=recv, device_id=device, device_id_type=MESH
        )

    def take(ref, sem):
        pltpu.make_async_copy(ref, ref, sem).wait()

    columns = pl.ds(pl.multiple_of(lev * HW, HW), HW)
    load_t = pltpu.make_async_copy(flux.at[:, :, columns], tbuf, ld.at[0])
    load_s = pltpu.make_async_copy(state, X.at[pl.ds(0, 5 * nk), pl.ds(0, ROWS), pl.ds(0, W)], ld.at[1])
    load_m = pltpu.make_async_copy(mask, mbuf, ld.at[2])
    load_t.start()
    load_s.start()
    load_m.start()

    barrier = pltpu.get_barrier_semaphore()

    def greet(device):
        pl.semaphore_signal(barrier, inc=1, device_id=device, device_id_type=MESH)

    def greet_plane(d, c):
        greet(plane((me + d) % NP))
        return c

    def greet_z(d, c):
        greet({"lon": ((z + d) % nz) * 2 + xl})
        return c

    lax.fori_loop(1, NP, greet_plane, 0)
    lax.fori_loop(1, nz, greet_z, 0)
    greet({"lev": other})
    for step in (1, nlon - 1):
        for l in (lev, other):
            greet({"lon": (lon + step) % nlon, "lev": l})

    @pl.when(jnp.logical_not(top))
    def _():
        greet({"lat": lat + 1, "lev": other})

    @pl.when(jnp.logical_not(bottom))
    def _():
        greet({"lat": lat - 1, "lev": other})

    @pl.when(top)
    def _():
        def greet_fold(d, c):
            greet({"lon": (lon + d) % nlon})
            greet({"lon": (lon + d) % nlon, "lev": other})
            return c

        lax.fori_loop(1, nlon, greet_fold, 0)

    owner, row = owner_ref[...], row_ref[...]
    eye = iota((tiles, tiles), 0) == iota((tiles, tiles), 1)
    upto = iota((tiles, tiles), 0) < iota((tiles, tiles), 1)
    wide = jnp.broadcast_to(owner, (tiles, tiles))
    col = jnp.sum(jnp.where(eye, wide, 0), axis=1, keepdims=True)
    slot = jnp.sum(jnp.where((col == wide) & upto, 1, 0), axis=0, keepdims=True)
    shift = int(math.log2(NP))
    to_p, to_z = owner & (NP - 1), owner >> shift
    target = to_p * (2 * nz) + slot * nz + to_z
    put = jnp.where(iota((N, tiles), 0) == target, 1.0, 0.0).astype(BF16)
    put3 = jnp.concatenate([put, put, put], axis=1)
    spot = jnp.where(iota((128, tiles), 0) == to_p * nz + to_z, 1.0, 0.0).astype(BF16)
    marks = jnp.where(iota((8, tiles), 0) == slot, (row + 1).astype(F32), 0.0).astype(BF16)
    meta[...] = lax.dot_general(marks, spot, (((1,), (1,)), ((), ())), preferred_element_type=F32)

    def pack(c):
        hi, mid, low = split3(tbuf[c])
        out = jnp.dot(put3, jnp.concatenate([hi, mid, low], axis=0), preferred_element_type=F32)
        pk[c] = out.reshape(NP, 2 * nz, HW)

    load_t.wait()
    pack(0)

    expected = (NP - 1) + (nz - 1) + 1 + 4
    extra = jnp.where(top, 2 * (nlon - 1), 1) + jnp.where(bottom, 0, 1)
    pl.semaphore_wait(barrier, expected + extra)

    def send_meta(d, c):
        p = (me + d) % NP
        remote(meta, metas.at[me], ms, mr, plane(p)).start()
        return c

    lax.fori_loop(1, NP, send_meta, 0)
    metas[me] = meta[...]

    def send_blocks(c):
        def one(d, carry):
            p = (me + d) % NP
            remote(pk.at[c, p], got.at[c, me], ss.at[c], sr.at[c], plane(p)).start()
            return carry

        lax.fori_loop(1, NP, one, 0)
        got[c, me] = pk[c, me]

    send_blocks(0)
    for c in (1, 2):
        pack(c)
        send_blocks(c)

    load_s.wait()
    load_m.wait()

    def wet(k, c):
        X[5 * nk + k, pl.ds(0, ROWS), pl.ds(0, W)] = mbuf[k].astype(F32)
        return c

    lax.fori_loop(0, nk, wet, 0)
    pair = iota((8, W), 0) // 2
    even = iota((8, W), 0) % 2 == 0

    def rows_out(g, c):
        low = jnp.zeros((8, W), F32)
        high = jnp.zeros((8, W), F32)
        is_mask = g >= (5 * nk) // 4
        for i in range(4):
            a = X[4 * g + i, pl.ds(0, 8), pl.ds(0, W)]
            b = X[4 * g + i, pl.ds(8, 8), pl.ds(0, W)]
            low = jnp.where(pair == i, pltpu.roll(a, 2 * i, 0), low)
            high = jnp.where(pair == i, pltpu.roll(b, (2 * i + 2) % 8, 0), high)
        hsend[0, g] = jnp.where(is_mask & jnp.logical_not(even), cor[0], low)
        hsend[1, g] = jnp.where(is_mask & even, cor[ROWS - 1], high)
        return c

    lax.fori_loop(0, nfk // 4, rows_out, 0)
    to_south = remote(hsend.at[0], hgot.at[0], hs.at[0], hr.at[0], {"lat": jnp.maximum(lat - 1, 0)})
    to_north = remote(hsend.at[1], hgot.at[1], hs.at[1], hr.at[1], {"lat": jnp.minimum(lat + 1, nlat - 1)})

    @pl.when(jnp.logical_not(bottom))
    def _():
        to_south.start()

    @pl.when(jnp.logical_not(top))
    def _():
        to_north.start()

    @pl.when(top)
    def _():
        shifted = hinge[0] % W
        for half_of in range(2):
            mirror[pl.ds(half_of * W, W), :] = jnp.where(
                iota((W, W), 0) + half_of * W == W + shifted - iota((W, W), 1), 1.0, 0.0
            ).astype(BF16)
        out = jnp.zeros((2 * nfk, W), F32)
        for lo, hi in zip(split3(fold_lo[...]), split3(fold_hi[...])):
            out += jnp.dot(lo, mirror[pl.ds(0, W), :], preferred_element_type=F32)
            out += jnp.dot(hi, mirror[pl.ds(W, W), :], preferred_element_type=F32)
        hgot[0] = out.reshape(nfk // 4, 8, W)

    @pl.when(bottom)
    def _():
        def fill(g, c):
            hgot[1, g] = pltpu.roll(hsend[0, g], 1, 0)
            return c

        lax.fori_loop(0, nfk // 4, fill, 0)

    take(metas.at[pl.ds(0, NP - 1)], mr)
    find = jnp.where(iota((128, N), 0) == me * nz + iota((128, N), 1) % nz, 1.0, 0.0).astype(BF16)
    known = jnp.dot(metas[...].reshape(NP * 8, 128).astype(BF16), find, preferred_element_type=F32)
    mine = iota((NP * 8, N), 1) // nz == (iota((NP * 8, N), 0) // 8) * 2 + iota((NP * 8, N), 0) % 8
    mine = mine & (iota((NP * 8, N), 0) % 8 < 2)
    named = jnp.sum(jnp.where(mine, known, 0.0), axis=0, keepdims=True)
    r_id = iota((nz * ROWS, N), 0)
    land = (r_id // ROWS == iota((nz * ROWS, N), 1) % nz) & ((r_id % ROWS + 1).astype(F32) == named)
    land = jnp.where(land, 1.0, 0.0).astype(BF16)
    land3 = jnp.concatenate([land, land, land], axis=1)

    def landed(c):
        take(got.at[c, pl.ds(0, NP - 1)], sr.at[c])
        hi, mid, low = split3(got[c].reshape(N, HW))
        out = jnp.dot(land3, jnp.concatenate([hi, mid, low], axis=0), preferred_element_type=F32)
        dense[c] = out.reshape(nz, ROWS, HW)

        def one(d, carry):
            t = (z + d) % nz
            remote(dense.at[c, t], zgot.at[c, z], zs.at[c], zr.at[c], {"lon": t * 2 + xl}).start()
            return carry

        lax.fori_loop(1, nz, one, 0)
        zgot[c, z] = dense[c, z]

    landed(0)

    @pl.when(jnp.logical_not(top))
    def _():
        to_south.wait_recv()

    @pl.when(jnp.logical_not(bottom))
    def _():
        to_north.wait_recv()

    upper = iota((8, W), 0) < 4

    def rows_in(g, c):
        n, s = hgot[0, g], hgot[1, g]
        for i in range(4):
            X[4 * g + i, pl.ds(ROWS, 8), pl.ds(0, W)] = jnp.where(
                upper, pltpu.roll(n, (8 - 2 * i) % 8, 0), pltpu.roll(s, (6 - 2 * i) % 8, 0)
            )
        return c

    lax.fori_loop(0, nfk // 4, rows_in, 0)
    lane = iota((EXT, 128), 1)

    def cols_out(f, c):
        w, e = c
        for k in range(nk):
            at = f * (2 * nk) + 2 * k
            a = X[f * nk + k, :, pl.ds(0, 128)]
            b = X[f * nk + k, :, pl.ds(W - 128, 128)]
            here = lane // 2 == f * nk + k
            w = jnp.where(here, pltpu.roll(a, at, 1), w)
            e = jnp.where(here, pltpu.roll(b, (at + 2) % 128, 1), e)
        return w, e

    w, e = lax.fori_loop(0, 6, cols_out, (jnp.zeros((EXT, 128), F32), jnp.zeros((EXT, 128), F32)))
    esend[0] = w
    esend[1] = e
    to_west = remote(esend.at[0], egot.at[0], es.at[0], er.at[0], {"lon": (lon + nlon - 1) % nlon})
    to_east = remote(esend.at[1], egot.at[1], es.at[1], er.at[1], {"lon": (lon + 1) % nlon})
    to_west.start()
    to_east.start()

    landed(1)

    to_west.wait_recv()
    to_east.wait_recv()
    fe, fw = egot[0], egot[1]

    def cols_in(f, c):
        for k in range(nk):
            at = f * (2 * nk) + 2 * k
            X[f * nk + k, :, pl.ds(W, 128)] = jnp.where(
                lane < 64, pltpu.roll(fe, (128 - at) % 128, 1), pltpu.roll(fw, (254 - at) % 128, 1)
            )
        return c

    lax.fori_loop(0, 6, cols_in, 0)

    to_lower = remote(levs, levg, ls, lr, {"lev": 1})
    to_lower2 = remote(lev2s, lev2g, ps, pr, {"lev": 1})

    @pl.when(lev == 0)
    def _():
        levs[...] = ALPHA * X[2 * nk] - BETA * X[3 * nk]

        def add(k, c):
            levs[...] += ALPHA * X[2 * nk + k] - BETA * X[3 * nk + k]
            return c

        lax.fori_loop(1, nk, add, 0)
        to_lower.start()
        levg[...] = jnp.zeros((EXT, WX), F32)

    row_id = iota((EXT, WX), 0)
    turning = jnp.where(row_id == ROWS, X[5 * nk, pl.ds(17, 1), :], X[5 * nk, pl.ds(22, 1), :])
    for i in range(ROWS):
        turning = jnp.where(row_id == i, cor[i], turning)
    cors[...] = turning

    landed(2)

    @pl.when(lev == 1)
    def _():
        to_lower.wait_recv()

    lev2s[...] = jnp.zeros((2, EXT, WX), F32)
    run = PX.at[0]
    run[...] = jnp.zeros((EXT, WX), F32)
    copy_row = (row_id == EXT - 1) & bottom

    def level(k, c):
        q = [X[f * nk + k] for f in range(5)]
        m = X[5 * nk + k]
        new, running = substep(q, m, levg[...], run[...], cors[...])
        run[...] = running
        new = [jnp.where(copy_row, a[0:1, :], a) for a in new]
        for f in range(5):
            X[f * nk + k] = new[f]
        lev2s[0] += ALPHA * new[2] - BETA * new[3]
        lev2s[1] += m * pen[k]
        return c

    lax.fori_loop(0, nk, level, 0)

    @pl.when(lev == 0)
    def _():
        to_lower2.start()
        lev2g[...] = jnp.zeros((2, EXT, WX), F32)

    for c in range(3):
        take(zgot.at[c, pl.ds(0, nz - 1)], zr.at[c])
        total = zgot[c, 0]
        for t in range(1, nz):
            total += zgot[c, t]
        half[c] = total
    for i, r in enumerate((0, ROWS - 1)):
        frow[i] = jnp.concatenate(
            [half[c, pl.ds(r, 1), pl.ds(q * 128, 128)] for c in range(3) for q in range(2)]
            + [jnp.zeros((2, 128), F32)],
            axis=0,
        )
    to_partner = remote(half, partner, ps2(rs, 0), ps2(rr, 0), {"lev": other})
    to_partner.start()
    south_at = jnp.maximum(lat - 1, 0)
    north_at = jnp.minimum(lat + 1, nlat - 1)
    down = [remote(frow.at[0], rowsgot.at[0, lev], rs.at[1 + i], rr.at[1 + i], {"lat": south_at, "lev": lev if i == 0 else other}) for i in range(2)]
    up = [remote(frow.at[1], rowsgot.at[1, lev], rs.at[3 + i], rr.at[3 + i], {"lat": north_at, "lev": lev if i == 0 else other}) for i in range(2)]

    @pl.when(jnp.logical_not(bottom))
    def _():
        for a in down:
            a.start()

    @pl.when(jnp.logical_not(top))
    def _():
        for a in up:
            a.start()

    edge = half.at[:, :, pl.ds(pl.multiple_of(lev * (HW - 128), 128), 128)]
    edge_to = (lon + nlon - 1 + 2 * lev) % nlon
    sides = [remote(edge, colsgot.at[lev], cs.at[i], cr.at[lev], {"lon": edge_to, "lev": lev if i == 0 else other}) for i in range(2)]
    for a in sides:
        a.start()

    @pl.when(top)
    def _():
        def one(d, c):
            for i in range(2):
                remote(
                    frow.at[1], foldgot.at[lev, lon], fs, fr.at[i],
                    {"lon": (lon + d) % nlon, "lev": lev if i == 0 else other},
                ).start()
            return c

        lax.fori_loop(1, nlon, one, 0)
        foldgot[lev, lon] = frow[1]

    FX[:, pl.ds(0, ROWS), pl.ds(pl.multiple_of(lev * HW, HW), HW)] = half[...]
    to_partner.wait_recv()
    FX[:, pl.ds(0, ROWS), pl.ds(pl.multiple_of(other * HW, HW), HW)] = partner[...]
    for i in range(2):
        pltpu.make_async_copy(colsgot.at[i], colsgot.at[i], cr.at[i]).wait()
    side = lax.broadcasted_iota(I32, (3, ROWS, 128), 2)
    FX[:, pl.ds(0, ROWS), pl.ds(W, 128)] = jnp.where(side < 64, colsgot[0], colsgot[1])

    first, last = iota((8, W), 0) == 0, iota((8, W), 0) == 7

    @pl.when(jnp.logical_not(bottom))
    def _():
        for i in range(2):
            up[i].wait_recv()

    @pl.when(jnp.logical_not(top))
    def _():
        for i in range(2):
            down[i].wait_recv()

    def joined(ref, c):
        return jnp.concatenate(
            [ref[h, pl.ds(2 * c + q, 1), pl.ds(0, 128)] for h in range(2) for q in range(2)], axis=1
        )

    @pl.when(top)
    def _():
        foldgot[other, lon] = jnp.concatenate(
            [partner[c, pl.ds(ROWS - 1, 1), pl.ds(q * 128, 128)] for c in range(3) for q in range(2)]
            + [jnp.zeros((2, 128), F32)],
            axis=0,
        )
        for i in range(2):
            take(foldgot.at[0, pl.ds(0, nlon - 1)], fr.at[i])
        b1 = (hinge[0] // W + nlon - lon) % nlon
        b0 = (b1 + nlon - 1) % nlon
        outs = [jnp.zeros((24, W), F32), jnp.zeros((24, W), F32)]
        for i, b in enumerate((b0, b1)):
            for h in range(2):
                tile = jnp.concatenate(split3(foldgot[h, b]), axis=0)
                for q in range(2):
                    at = i * W + h * HW + q * 128
                    keep = jnp.where(iota((24, 128), 0) % 2 == q, tile.astype(F32), 0.0).astype(BF16)
                    outs[q] += jnp.dot(keep, mirror[pl.ds(at, 128), :], preferred_element_type=F32)
        sums = [o[0:8] + o[8:16] + o[16:24] for o in outs]
        for c in range(3):
            rowsgot2(FX, c, sums[0][2 * c : 2 * c + 1] + sums[1][2 * c + 1 : 2 * c + 2], first, W)

    @pl.when(jnp.logical_not(top))
    def _():
        for c in range(3):
            rowsgot2(FX, c, joined(rowsgot.at[0], c), first, W)

    @pl.when(bottom)
    def _():
        for c in range(3):
            FX[c, pl.ds(ROWS, 8), pl.ds(0, W)] = jnp.where(
                last, FX[c, pl.ds(0, 1), pl.ds(0, W)], FX[c, pl.ds(ROWS, 8), pl.ds(0, W)]
            )

    @pl.when(jnp.logical_not(bottom))
    def _():
        for c in range(3):
            FX[c, pl.ds(ROWS, 8), pl.ds(0, W)] = jnp.where(
                last, joined(rowsgot.at[1], c), FX[c, pl.ds(ROWS, 8), pl.ds(0, W)]
            )

    FX[:, pl.ds(ROWS, 8), pl.ds(W, 128)] = jnp.zeros((3, 8, 128), F32)

    @pl.when(lev == 1)
    def _():
        to_lower2.wait_recv()

    PX[...] = lev2g[...]

    take(metas.at[pl.ds(0, NP - 1)], ms)
    for c in range(3):
        take(pk.at[c, pl.ds(0, NP - 1)], ss.at[c])
        take(dense.at[c, pl.ds(0, nz - 1)], zs.at[c])
    to_west.wait_send()
    to_east.wait_send()
    to_partner.wait_send()
    for a in sides:
        a.wait_send()

    @pl.when(lev == 0)
    def _():
        to_lower.wait_send()
        to_lower2.wait_send()

    @pl.when(jnp.logical_not(bottom))
    def _():
        to_south.wait_send()
        for a in down:
            a.wait_send()

    @pl.when(jnp.logical_not(top))
    def _():
        to_north.wait_send()
        for a in up:
            a.wait_send()

    @pl.when(top)
    def _():
        take(foldgot.at[:, pl.ds(0, nlon - 1)], fs)


def ps2(ref, i):
    return ref.at[i]


def rowsgot2(FX, c, line, first, W):
    FX[c, pl.ds(ROWS, 8), pl.ds(0, W)] = jnp.where(first, line, 0.0)


def finish_kernel(nk, W, X, FX, PX, cor, pen, out, run):
    k = pl.program_id(0)
    WX = W + 128
    row_id = iota((EXT, WX), 0)

    @pl.when(k == 0)
    def _():
        run[0] = jnp.zeros((EXT, WX), F32)
        extra = ALPHA * FX[0] - BETA * FX[1]
        run[1] = PX[0] + PX[1] * extra
        turning = jnp.zeros((EXT, WX), F32)
        for i in range(ROWS):
            turning = jnp.where(row_id == i, cor[i], turning)
        run[2] = turning

    m = X[5, 0]
    gain = m * pen[k]
    push = [gain * FX[c] for c in range(3)]
    q = [X[f, 0] + push[f - 2] if f > 1 else X[f, 0] for f in range(5)]
    new, running = substep(q, m, run[1], run[0], run[2])
    run[0] = running
    for f in range(5):
        result = new[f] + push[f - 2] if f > 1 else new[f]
        out[f, 0] = result[0:ROWS, 0:W]


def body(state, mask, coriolis, penetration, flux_tiles, flux_owner, flux_row, fold_partner):
    _, nk, rows, W = state.shape
    nlon, nlat = lax.axis_size("lon"), lax.axis_size("lat")
    tiles = flux_tiles.shape[0]
    nz, NP = nlon // 2, 2 * nlat
    N, HW, WX, nfk = NP * 2 * nz, W // 2, W + 128, 6 * nk
    hinge = fold_partner[0:1]

    with jax.named_scope("fold_rows"):
        signs = jnp.array([-1.0, -1.0, 1.0, 1.0, 1.0], F32)[:, None, None, None]
        pair = jnp.concatenate([state[:, :, rows - 1 :], state[:, :, rows - 2 : rows - 1]], axis=2) * signs
        wet = mask[:, rows - 1 :].astype(F32)
        wet = jnp.concatenate([wet, jnp.full_like(wet, coriolis[rows - 1])], axis=1)
        pair = jnp.concatenate([pair, wet[None]], axis=0).reshape(2 * nfk, W)

        def turned(block, value):
            at = lambda i: i * nlat + nlat - 1
            high = [(at(i), at((block - i) % nlon)) for i in range(nlon)]
            low = [(at(i), at((block - 1 - i) % nlon)) for i in range(nlon)]
            return lax.ppermute(value, ("lon", "lat"), low), lax.ppermute(value, ("lon", "lat"), high)

        fold_lo, fold_hi = lax.switch(hinge[0] // W, [functools.partial(turned, b) for b in range(nlon)], pair)

    vmem, smem, hbm = (pl.BlockSpec(memory_space=s) for s in (pltpu.VMEM, pltpu.SMEM, pl.ANY))
    V = lambda *s: pltpu.VMEM(s, F32)
    D = lambda *s: pltpu.SemaphoreType.DMA(s)
    X, FX, PX = pl.pallas_call(
        functools.partial(exchange_kernel, nlon, nlat, tiles, nk, W),
        out_shape=(
            jax.ShapeDtypeStruct((nfk, EXT, WX), F32),
            jax.ShapeDtypeStruct((3, EXT, WX), F32),
            jax.ShapeDtypeStruct((2, EXT, WX), F32),
        ),
        in_specs=[hbm, hbm, smem, smem, hbm, vmem, vmem, smem, vmem, vmem],
        out_specs=(vmem, vmem, vmem),
        scratch_shapes=[
            V(3, tiles, HW), pltpu.VMEM((nk, ROWS, W), I32),
            V(3, NP, 2 * nz, HW), V(3, NP, 2 * nz, HW), V(8, 128), V(NP, 8, 128),
            V(3, nz, ROWS, HW), V(3, nz, ROWS, HW), V(3, ROWS, HW), V(3, ROWS, HW),
            V(2, 8, 128), V(2, 2, 8, 128), V(2, 3, ROWS, 128), V(2, nlon, 8, 128),
            V(2, nfk // 4, 8, W), V(2, nfk // 4, 8, W), V(2, EXT, 128), V(2, EXT, 128),
            V(EXT, WX), V(EXT, WX), V(2, EXT, WX), V(2, EXT, WX), V(EXT, WX), pltpu.VMEM((2 * W, W), BF16),
            D(3), pltpu.SemaphoreType.DMA, pltpu.SemaphoreType.DMA, D(3), D(3), D(3), D(3), D(2), D(2), D(2), D(2),
            pltpu.SemaphoreType.DMA, pltpu.SemaphoreType.DMA, pltpu.SemaphoreType.DMA, pltpu.SemaphoreType.DMA,
            D(5), D(5), D(2), D(2), pltpu.SemaphoreType.DMA, D(2),
        ],
        compiler_params=pltpu.CompilerParams(
            collective_id=0, has_side_effects=True, vmem_limit_bytes=40 * 1024 * 1024
        ),
        name="exchange",
    )(
        state.reshape(5 * nk, rows, W), mask, coriolis, penetration, flux_tiles.transpose(1, 0, 2),
        flux_owner.reshape(1, tiles), flux_row.reshape(1, tiles), hinge, fold_lo, fold_hi,
    )

    return pl.pallas_call(
        functools.partial(finish_kernel, nk, W),
        grid=(nk,),
        out_shape=jax.ShapeDtypeStruct(state.shape, F32),
        in_specs=[
            pl.BlockSpec((6, 1, EXT, WX), lambda k: (0, k, 0, 0)),
            pl.BlockSpec((3, EXT, WX), lambda k: (0, 0, 0)),
            pl.BlockSpec((2, EXT, WX), lambda k: (0, 0, 0)),
            smem,
            smem,
        ],
        out_specs=pl.BlockSpec((5, 1, rows, W), lambda k: (0, k, 0, 0)),
        scratch_shapes=[V(3, EXT, WX)],
        compiler_params=pltpu.CompilerParams(vmem_limit_bytes=32 * 1024 * 1024),
        name="finish",
    )(X.reshape(6, nk, EXT, WX), FX, PX, coriolis, penetration)


def solution(mesh):
    return jax.shard_map(
        body,
        mesh=mesh,
        in_specs=(
            P(None, "lev", "lat", "lon"),
            P("lev", "lat", "lon"),
            P("lat"),
            P("lev"),
            P(("lon", "lat"), None, None),
            P(("lon", "lat"), None),
            P(("lon", "lat")),
            P(),
        ),
        out_specs=P(None, "lev", "lat", "lon"),
        check_vma=False,
    )
```

time: 296 us -> 69.7 us (0.24)
  the two profiles are of different devices: /device:TPU:4 before, /device:TPU:1 now
where the time goes in v1:
time: 69.7 us; the launch traced here: 69.4 us
  Pallas kernels  57.2 us (82%)
  local copies, waits for them, and re-layouts  6 us (9%)
  between operations  2.77 us (4%)
  starting transfers between devices  2.67 us (4%)
  other arithmetic  0.76 us (1%)
    pallas_call x1, Pallas kernels, body(): pl.pallas_call(functools.partial(exchange_kernel, nlon, nlat, tiles, nk,...  52.6 us
    pallas_call x1, Pallas kernels, body(): pl.pallas_call(functools.partial(finish_kernel, nk, W), grid=(nk,), out_s...  4.61 us
    slice x1, local copies, waits for them, and re-layouts, body(): state[:, :, rows - 1:]  1.49 us
    slice x1, local copies, waits for them, and re-layouts, body(): wet = jnp.concatenate([wet, jnp.full_like(wet, coriolis[rows - 1])], axis=1)  1.41 us
  transfers between devices with their start and end apart: 2, of which 0 were waited for; matrix products, arithmetic and copies ran while one was open for 0% of the time, Pallas kernels for 0%

profile of v1, /device:TPU:1, one launch (start us, length us, event | category | flops | bytes accessed | tf_op | source)
XLA Modules:
  0.0 69.4 jit_solution(7571633658654787889)
XLA Ops:
  0.0 0.0 copy-start.3
  0.0 0.0 copy-start.4
  0.0 0.0 copy-start.2
  0.0 0.0 copy-start
  0.0 0.0 copy-start.6
  0.0 0.0 copy-start.5
  0.0 0.0 copy-start.1
  0.1 1.4 %slice.19 = f32[1]{0:T(128)} slice(f32[16]{0:T(128)} %cor.3), slice={[15:16]} | slice | bytes 8 | tf_op jit(solution)/shard_map/fold_rows/slice | solution.py:573
  1.5 1.2 %slice.15.hinge = s32[1]{0:T(128)} slice(s32[8192]{0:T(1024)} %param.32), slice={[0:1]} | slice | bytes 8 | tf_op jit(solution)/shard_map/slice | solution.py:567
  5.3 0.9 %slice.18 = s32[8,1,512]{2,1,0:T(1,128)S(1)} slice(s32[8,16,512]{2,1,0:T(8,128)} %mask.1), slice={[0:8], [15:16], [0:512]} | slice | bytes 32768 | tf_op jit(solution)/shard_map/fold_rows/slice | solution.py:572
  6.2 0.6 pad_bitcast_fusion
  6.9 1.5 %fusion = (f32[5,8,1,512]{3,2,1,0:T(1,128)S(1)}, f32[5,8,1,512]{3,2,1,0:T(1,128)S(1)}) fusion(f32[5,8,16,512]{3,2,1,0:T(8,128)} %param.25), kind=kLoop, calls=%fused_computation.4 | loop fusion | bytes 327680 | tf_op jit(solution)/shard_map/fold_rows/slice | solution.py:571
  8.4 0.7 %maximum_multiply_fusion = f32[5,8,2,512]{3,1,2,0:T(8,128)S(1)} fusion(f32[5,8,1,512]{3,1,2,0:T(8,128)S(1)} %copy.15, f32[5,8,1,512]{3,1,2,0:T(8,128)S(1)} %copy.14, f32[5]{0:T(128)} %constant.21.clone), kind=kLoop, calls=%fused_computation.1 | loop fusion | flops 81920 | bytes 327700 | tf_op jit(solution)/shard_map/fold_rows/mul | solution.py:571
  9.1 0.2 copy.13
  9.3 0.1 reshape.67
  9.5 2.7 %conditional.1 = (f32[96,512]{1,0:T(8,128)}, f32[96,512]{1,0:T(8,128)}) conditional(s32[]{:T(128)} %clamp.3, f32[96,512]{1,0:T(8,128)S(1)} %reshape.67, f32[96,512]{1,0:T(8,128)S(1)} %reshape.67, f32[96,512]{1,0:T(8,128)S(1)} %reshape.67, f32[96,512]{1,0:T(8,128)S(1)} %reshape.67, ...), branch_computations={%region_0.1_spmd, %region_1.2_spmd, %region_2.3_spmd, %region_3.4_... | conditional | bytes 1572960 | solution.py:582
  9.5 1.3 %collective-permute-start.1 = (f32[96,512]{1,0:T(8,128)S(1)}, f32[96,512]{1,0:T(8,128)}, u32[]{:S(2)}, u32[]{:S(2)}) collective-permute-start(f32[96,512]{1,0:T(8,128)S(1)} %param), channel_id=1, source_target_pairs={{14,14},{30,254},{46,238},{62,222},{78,206},{94,190},{110,174},{12... | collective-permute-start | bytes 589832 | tf_op jit(solution)/shard_map/fold_rows/cond/branch_0_fun/ppermute | solution.py:580
  10.8 1.3 %collective-permute-start = (f32[96,512]{1,0:T(8,128)S(1)}, f32[96,512]{1,0:T(8,128)}, u32[]{:S(2)}, u32[]{:S(2)}) collective-permute-start(f32[96,512]{1,0:T(8,128)S(1)} %param), channel_id=1, source_target_pairs={{14,254},{30,238},{46,222},{62,206},{78,190},{94,174},{110,158},{1... | collective-permute-start | bytes 589832 | tf_op jit(solution)/shard_map/fold_rows/cond/branch_0_fun/ppermute | solution.py:580
  12.1 0.0 collective-permute-done.1
  12.1 0.0 collective-permute-done
  12.1 0.0 copy-done.3
  12.2 0.0 copy-done.4
  12.2 0.0 copy-done.2
  12.2 0.0 copy-done
  12.2 0.0 copy-done.6
  12.2 0.0 copy-done.5
  12.2 0.0 copy-done.1
  12.2 52.6 %exchange.1 = (f32[48,24,640]{2,1,0:T(8,128)S(1)}, f32[3,24,640]{2,1,0:T(8,128)S(1)}, f32[2,24,640]{2,1,0:T(8,128)S(1)}) custom-call(f32[40,16,512]{2,1,0:T(8,128)S(1)} %bitcast.10, s32[8,16,512]{2,1,0:T(8,128)S(1)} %copy-done.2, f32[16]{0:T(128)S(1)} %copy-done.3, f32[8]{0:T(128)S(1)} %copy-done.4, f32[3,128,512]{2,1,0:T(8,128)S(1)} %bitcast.11, ...), custom_call_target="tpu_custom_call" | custom-call | tf_op jit(solution)/shard_map/exchange/pallas_call | solution.py:587
  64.8 4.6 %finish.1 = f32[5,8,16,512]{3,2,1,0:T(8,128)} custom-call(f32[6,8,24,640]{3,2,1,0:T(8,128)S(1)} %bitcast.9, f32[3,24,640]{2,1,0:T(8,128)S(1)} %get-tuple-element.29.FX, f32[2,24,640]{2,1,0:T(8,128)S(1)} %get-tuple-element.30.PX, f32[16]{0:T(128)S(1)} %copy-done.3, f32[8]{0:T(128)S(1)} %copy-done.4), custom_call_target="tpu_custom_call" | custom-call | tf_op jit(solution)/shard_map/finish/pallas_call | solution.py:616
  (4 shorter events, 0.0 us)
Async XLA Ops:
  0.0 12.1 %copy-start.3 = (f32[16]{0:T(128)S(1)}, f32[16]{0:T(128)}, u32[]{:S(2)}) copy-start(f32[16]{0:T(128)} %cor.3) | copy-start | bytes 196
  0.0 12.2 %copy-start.4 = (f32[8]{0:T(128)S(1)}, f32[8]{0:T(128)}, u32[]{:S(2)}) copy-start(f32[8]{0:T(128)} %pen.3) | copy-start | bytes 100
  0.0 12.2 %copy-start.2 = (s32[8,16,512]{2,1,0:T(8,128)S(1)}, s32[8,16,512]{2,1,0:T(8,128)}, u32[]{:S(2)}) copy-start(s32[8,16,512]{2,1,0:T(8,128)} %mask.1) | copy-start | bytes 786436
  0.0 12.2 %copy-start = (f32[5,8,16,512]{3,2,1,0:T(8,128)S(1)}, f32[5,8,16,512]{3,2,1,0:T(8,128)}, u32[]{:S(2)}) copy-start(f32[5,8,16,512]{3,2,1,0:T(8,128)} %param.25) | copy-start | bytes 3932164
  0.0 12.2 %copy-start.6 = (s32[128]{0:T(128)S(1)}, s32[128]{0:T(128)}, u32[]{:S(2)}) copy-start(s32[128]{0:T(128)} %param.31) | copy-start | bytes 1540
  0.0 12.2 %copy-start.5 = (s32[128,1]{0,1:T(1,128)S(1)}, s32[128,1]{0,1:T(1,128)}, u32[]{:S(2)}) copy-start(s32[128,1]{0,1:T(1,128)} %param.30) | copy-start | bytes 1540
  0.0 12.2 %copy-start.1 = (f32[128,3,512]{2,0,1:T(8,128)S(1)}, f32[128,3,512]{2,0,1:T(8,128)}, u32[]{:S(2)}) copy-start(f32[128,3,512]{2,0,1:T(8,128)} %param.29) | copy-start | bytes 2359300
  9.5 2.7 %collective-permute-start.1 = (f32[96,512]{1,0:T(8,128)S(1)}, f32[96,512]{1,0:T(8,128)}, u32[]{:S(2)}, u32[]{:S(2)}) collective-permute-start(f32[96,512]{1,0:T(8,128)S(1)} %param), channel_id=1, source_target_pairs={{14,14},{30,254},{46,238},{62,222},{78,206},{94,190},{110,174},{12... | collective-permute-start | bytes 589832 | tf_op jit(solution)/shard_map/fold_rows/cond/branch_0_fun/ppermute | solution.py:580
  10.8 1.3 %collective-permute-start = (f32[96,512]{1,0:T(8,128)S(1)}, f32[96,512]{1,0:T(8,128)}, u32[]{:S(2)}, u32[]{:S(2)}) collective-permute-start(f32[96,512]{1,0:T(8,128)S(1)} %param), channel_id=1, source_target_pairs={{14,254},{30,238},{46,222},{62,206},{78,190},{94,174},{110,158},{1... | collective-permute-start | bytes 589832 | tf_op jit(solution)/shard_map/fold_rows/cond/branch_0_fun/ppermute | solution.py:580

commit v2 on v1

--- a/solution.py
+++ b/solution.py
@@ -56,11 +56,11 @@
 
 def exchange_kernel(
     nlon, nlat, tiles, nk, W,
-    state, mask, cor, pen, flux, owner_ref, row_ref, hinge, fold_lo, fold_hi,
+    state, mask, cor_hbm, pen_hbm, flux, owner_hbm, row_hbm, columns_ref,
     X, FX, PX,
-    tbuf, mbuf, pk, got, meta, metas, dense, zgot, half, partner, frow, rowsgot, colsgot, foldgot,
-    hsend, hgot, esend, egot, levs, levg, lev2s, lev2g, cors, mirror,
-    ld, ms, mr, ss, sr, zs, zr, hs, hr, es, er, ls, lr, ps, pr, rs, rr, cs, cr, fs, fr,
+    tbuf, mbuf, pk, got, meta, metas, dense, east_out, east_in, west_out, west_in, half, partner, frow, rowsgot, colsgot, foldgot,
+    hsend, hgot, fold, folda, foldm, foldb, fold_rows, hinge, cor, pen, owner_ref, row_ref, esend, egot, levs, levg, lev2s, lev2g, cors, mirror,
+    ld, ms, mr, ss, sr, zes, zer, zws, zwr, hs, hr, es, er, ls, lr, ps, pr, rs, rr, cs, cr, fs, fr, gas, gar, gbs, gbr,
 ):
     lon, lat, lev = lax.axis_index("lon"), lax.axis_index("lat"), lax.axis_index("lev")
     nz, NP = nlon // 2, 2 * nlat
@@ -91,6 +91,14 @@
     load_t.start()
     load_s.start()
     load_m.start()
+    smalls = [
+        pltpu.make_async_copy(a, b, ld.at[4 + i])
+        for i, (a, b) in enumerate(((owner_hbm, owner_ref), (row_hbm, row_ref), (cor_hbm, cor), (pen_hbm, pen)))
+    ]
+    for a in smalls:
+        a.start()
+    load_h = pltpu.make_async_copy(columns_ref.at[pl.ds(0, 1024)], hinge, ld.at[3])
+    load_h.start()
 
     barrier = pltpu.get_barrier_semaphore()
 
@@ -101,12 +109,10 @@
         greet(plane((me + d) % NP))
         return c
 
-    def greet_z(d, c):
-        greet({"lon": ((z + d) % nz) * 2 + xl})
-        return c
-
     lax.fori_loop(1, NP, greet_plane, 0)
-    lax.fori_loop(1, nz, greet_z, 0)
+    up_z, down_z = {"lon": ((z + 1) % nz) * 2 + xl}, {"lon": ((z + nz - 1) % nz) * 2 + xl}
+    greet(up_z)
+    greet(down_z)
     greet({"lev": other})
     for step in (1, nlon - 1):
         for l in (lev, other):
@@ -129,6 +135,8 @@
 
         lax.fori_loop(1, nlon, greet_fold, 0)
 
+    for a in smalls:
+        a.wait()
     owner, row = owner_ref[...], row_ref[...]
     eye = iota((tiles, tiles), 0) == iota((tiles, tiles), 1)
     upto = iota((tiles, tiles), 0) < iota((tiles, tiles), 1)
@@ -152,32 +160,6 @@
     load_t.wait()
     pack(0)
 
-    expected = (NP - 1) + (nz - 1) + 1 + 4
-    extra = jnp.where(top, 2 * (nlon - 1), 1) + jnp.where(bottom, 0, 1)
-    pl.semaphore_wait(barrier, expected + extra)
-
-    def send_meta(d, c):
-        p = (me + d) % NP
-        remote(meta, metas.at[me], ms, mr, plane(p)).start()
-        return c
-
-    lax.fori_loop(1, NP, send_meta, 0)
-    metas[me] = meta[...]
-
-    def send_blocks(c):
-        def one(d, carry):
-            p = (me + d) % NP
-            remote(pk.at[c, p], got.at[c, me], ss.at[c], sr.at[c], plane(p)).start()
-            return carry
-
-        lax.fori_loop(1, NP, one, 0)
-        got[c, me] = pk[c, me]
-
-    send_blocks(0)
-    for c in (1, 2):
-        pack(c)
-        send_blocks(c)
-
     load_s.wait()
     load_m.wait()
 
@@ -200,9 +182,41 @@
             high = jnp.where(pair == i, pltpu.roll(b, (2 * i + 2) % 8, 0), high)
         hsend[0, g] = jnp.where(is_mask & jnp.logical_not(even), cor[0], low)
         hsend[1, g] = jnp.where(is_mask & even, cor[ROWS - 1], high)
+        sign = jnp.where(g < (2 * nk) // 4, -1.0, 1.0)
+        turned = sign * jnp.where(even, pltpu.roll(high, 7, 0), pltpu.roll(high, 1, 0))
+        fold[g] = jnp.where(is_mask & jnp.logical_not(even), cor[ROWS - 1], turned)
         return c
 
     lax.fori_loop(0, nfk // 4, rows_out, 0)
+    expected = (NP - 1) + 2 + 1 + 4
+    extra = jnp.where(top, 2 * (nlon - 1), 1) + jnp.where(bottom, 0, 1)
+    pl.semaphore_wait(barrier, expected + extra)
+
+    spread = (-2, -1, 1, 2)
+    there = [(4 * a + nlon - lon) % nlon for a in range(4)]
+    first_hop = [remote(fold, folda.at[a], gas.at[a], gar.at[a], {"lon": there[a]}) for a in range(4)]
+    second_hop = [
+        remote(foldm, foldb.at[b + 2], gbs.at[i], gbr.at[i], {"lon": (lon + b + nlon) % nlon})
+        for i, b in enumerate(spread)
+    ]
+
+    edge_of = pl.ds(0, 128)
+    third_hop = remote(
+        foldm.at[:, :, edge_of], foldb.at[5, :, :, edge_of], gbs.at[4], gbr.at[4], {"lon": (lon + 3) % nlon}
+    )
+
+    @pl.when(top)
+    def _():
+        for a in range(4):
+
+            @pl.when(there[a] != lon)
+            def _():
+                first_hop[a].start()
+
+            @pl.when(there[a] == lon)
+            def _():
+                folda[a] = fold[...]
+
     to_south = remote(hsend.at[0], hgot.at[0], hs.at[0], hr.at[0], {"lat": jnp.maximum(lat - 1, 0)})
     to_north = remote(hsend.at[1], hgot.at[1], hs.at[1], hr.at[1], {"lat": jnp.minimum(lat + 1, nlat - 1)})
 
@@ -214,18 +228,48 @@
     def _():
         to_north.start()
 
+
+    def send_meta(d, c):
+        p = (me + d) % NP
+        remote(meta, metas.at[me], ms, mr, plane(p)).start()
+        return c
+
+    lax.fori_loop(1, NP, send_meta, 0)
+    metas[me] = meta[...]
+
+    def send_blocks(c):
+        def one(d, carry):
+            p = (me + d) % NP
+            remote(pk.at[c, p], got.at[c, me], ss.at[c], sr.at[c], plane(p)).start()
+            return carry
+
+        lax.fori_loop(1, NP, one, 0)
+        got[c, me] = pk[c, me]
+
+    send_blocks(0)
+    for c in (1, 2):
+        pack(c)
+        send_blocks(c)
+
+    load_h.wait()
+    block, shifted = hinge[0] // W, hinge[0] % W
+    digit = (block + 1) // 4
+
     @pl.when(top)
     def _():
-        shifted = hinge[0] % W
-        for half_of in range(2):
-            mirror[pl.ds(half_of * W, W), :] = jnp.where(
-                iota((W, W), 0) + half_of * W == W + shifted - iota((W, W), 1), 1.0, 0.0
+        at = iota((W, WX), 1)
+        at = jnp.where(at < W + 64, at, at - WX)
+        for i in range(3):
+            wide = W if i < 2 else 128
+            mirror[pl.ds(i * W, wide), :] = jnp.where(
+                iota((wide, WX), 0) + i * W == W + shifted - at[0:wide], 1.0, 0.0
             ).astype(BF16)
-        out = jnp.zeros((2 * nfk, W), F32)
-        for lo, hi in zip(split3(fold_lo[...]), split3(fold_hi[...])):
-            out += jnp.dot(lo, mirror[pl.ds(0, W), :], preferred_element_type=F32)
-            out += jnp.dot(hi, mirror[pl.ds(W, W), :], preferred_element_type=F32)
-        hgot[0] = out.reshape(nfk // 4, 8, W)
+
+        def clear(g, c):
+            hgot[0, g] = jnp.zeros((8, W), F32)
+            return c
+
+        lax.fori_loop(0, nfk // 4, clear, 0)
 
     @pl.when(bottom)
     def _():
@@ -246,21 +290,34 @@
     land = jnp.where(land, 1.0, 0.0).astype(BF16)
     land3 = jnp.concatenate([land, land, land], axis=1)
 
+    ahead = nz // 2
+    behind = nz - 1 - ahead
+
+    def hop(c, s, up):
+        out, into, send, recv, to = (
+            (east_out, east_in, zes, zer, up_z) if up else (west_out, west_in, zws, zwr, down_z)
+        )
+        return remote(out.at[c, s], into.at[c, s], send.at[c, s], recv.at[c, s], to)
+
+    def ring(c, s):
+        for up, steps in ((True, ahead), (False, behind)):
+            if s >= steps:
+                continue
+            out, into = (east_out, east_in) if up else (west_out, west_in)
+            block = dense[c, (z + (steps - s if up else nz - steps + s)) % nz]
+            if s > 0:
+                hop(c, s - 1, up).wait_recv()
+                block += into[c, s - 1]
+            out[c, s] = block
+            hop(c, s, up).start()
+
     def landed(c):
         take(got.at[c, pl.ds(0, NP - 1)], sr.at[c])
         hi, mid, low = split3(got[c].reshape(N, HW))
         out = jnp.dot(land3, jnp.concatenate([hi, mid, low], axis=0), preferred_element_type=F32)
         dense[c] = out.reshape(nz, ROWS, HW)
 
-        def one(d, carry):
-            t = (z + d) % nz
-            remote(dense.at[c, t], zgot.at[c, z], zs.at[c], zr.at[c], {"lon": t * 2 + xl}).start()
-            return carry
-
-        lax.fori_loop(1, nz, one, 0)
-        zgot[c, z] = dense[c, z]
-
-    landed(0)
+        ring(c, 0)
 
     @pl.when(jnp.logical_not(top))
     def _():
@@ -302,8 +359,8 @@
     to_west.start()
     to_east.start()
 
-    landed(1)
-
+    for c in range(3):
+        landed(c)
     to_west.wait_recv()
     to_east.wait_recv()
     fe, fw = egot[0], egot[1]
@@ -318,62 +375,37 @@
 
     lax.fori_loop(0, 6, cols_in, 0)
 
-    to_lower = remote(levs, levg, ls, lr, {"lev": 1})
-    to_lower2 = remote(lev2s, lev2g, ps, pr, {"lev": 1})
-
-    @pl.when(lev == 0)
-    def _():
-        levs[...] = ALPHA * X[2 * nk] - BETA * X[3 * nk]
-
-        def add(k, c):
-            levs[...] += ALPHA * X[2 * nk + k] - BETA * X[3 * nk + k]
+    for c in range(3):
+        ring(c, 1)
+
+    @pl.when(top)
+    def _():
+        for a in range(4):
+
+            @pl.when(there[a] != lon)
+            def _():
+                first_hop[a].wait_recv()
+
+        def pick(g, c):
+            foldm[g] = folda[digit % 4, g]
+            foldb[2, g] = folda[digit % 4, g]
             return c
 
-        lax.fori_loop(1, nk, add, 0)
-        to_lower.start()
-        levg[...] = jnp.zeros((EXT, WX), F32)
-
-    row_id = iota((EXT, WX), 0)
-    turning = jnp.where(row_id == ROWS, X[5 * nk, pl.ds(17, 1), :], X[5 * nk, pl.ds(22, 1), :])
-    for i in range(ROWS):
-        turning = jnp.where(row_id == i, cor[i], turning)
-    cors[...] = turning
-
-    landed(2)
-
-    @pl.when(lev == 1)
-    def _():
-        to_lower.wait_recv()
-
-    lev2s[...] = jnp.zeros((2, EXT, WX), F32)
-    run = PX.at[0]
-    run[...] = jnp.zeros((EXT, WX), F32)
-    copy_row = (row_id == EXT - 1) & bottom
-
-    def level(k, c):
-        q = [X[f * nk + k] for f in range(5)]
-        m = X[5 * nk + k]
-        new, running = substep(q, m, levg[...], run[...], cors[...])
-        run[...] = running
-        new = [jnp.where(copy_row, a[0:1, :], a) for a in new]
-        for f in range(5):
-            X[f * nk + k] = new[f]
-        lev2s[0] += ALPHA * new[2] - BETA * new[3]
-        lev2s[1] += m * pen[k]
-        return c
-
-    lax.fori_loop(0, nk, level, 0)
-
-    @pl.when(lev == 0)
-    def _():
-        to_lower2.start()
-        lev2g[...] = jnp.zeros((2, EXT, WX), F32)
+        lax.fori_loop(0, nfk // 4, pick, 0)
+        for a in second_hop:
+            a.start()
+        third_hop.start()
+
+    for s in range(2, ahead):
+        for c in range(3):
+            ring(c, s)
 
     for c in range(3):
-        take(zgot.at[c, pl.ds(0, nz - 1)], zr.at[c])
-        total = zgot[c, 0]
-        for t in range(1, nz):
-            total += zgot[c, t]
+        hop(c, ahead - 1, True).wait_recv()
+        total = dense[c, z] + east_in[c, ahead - 1]
+        if behind:
+            hop(c, behind - 1, False).wait_recv()
+            total += west_in[c, behind - 1]
         half[c] = total
     for i, r in enumerate((0, ROWS - 1)):
         frow[i] = jnp.concatenate(
@@ -417,6 +449,79 @@
         lax.fori_loop(1, nlon, one, 0)
         foldgot[lev, lon] = frow[1]
 
+    @pl.when(top)
+    def _():
+        for a in second_hop:
+            a.wait_recv()
+        third_hop.wait_recv()
+        near = block - 4 * digit + 1
+        out = jnp.zeros((2 * nfk, WX), F32)
+        for i in range(3):
+            wide = W if i < 2 else 128
+            for part in split3(foldb[near + i, :, :, pl.ds(0, wide)].reshape(2 * nfk, wide)):
+                out += jnp.dot(part, mirror[pl.ds(i * W, wide), :], preferred_element_type=F32)
+        fold_rows[...] = out.reshape(nfk // 4, 8, WX)
+        two = iota((8, WX), 0) < 2
+
+        def insert(g, c):
+            n = fold_rows[g]
+            for i in range(4):
+                X[4 * g + i, pl.ds(ROWS, 8), :] = jnp.where(
+                    two, pltpu.roll(n, (8 - 2 * i) % 8, 0), X[4 * g + i, pl.ds(ROWS, 8), :]
+                )
+            return c
+
+        lax.fori_loop(0, nfk // 4, insert, 0)
+
+    to_lower = remote(levs, levg, ls, lr, {"lev": 1})
+    to_lower2 = remote(lev2s, lev2g, ps, pr, {"lev": 1})
+
+    @pl.when(lev == 0)
+    def _():
+        levs[...] = ALPHA * X[2 * nk] - BETA * X[3 * nk]
+
+        def add(k, c):
+            levs[...] += ALPHA * X[2 * nk + k] - BETA * X[3 * nk + k]
+            return c
+
+        lax.fori_loop(1, nk, add, 0)
+        to_lower.start()
+        levg[...] = jnp.zeros((EXT, WX), F32)
+
+    row_id = iota((EXT, WX), 0)
+    turning = jnp.where(row_id == ROWS, X[5 * nk, pl.ds(17, 1), :], X[5 * nk, pl.ds(22, 1), :])
+    for i in range(ROWS):
+        turning = jnp.where(row_id == i, cor[i], turning)
+    cors[...] = turning
+
+    @pl.when(lev == 1)
+    def _():
+        to_lower.wait_recv()
+
+    lev2s[...] = jnp.zeros((2, EXT, WX), F32)
+    run = PX.at[0]
+    run[...] = jnp.zeros((EXT, WX), F32)
+    copy_row = (row_id == EXT - 1) & bottom
+
+    def level(k, c):
+        q = [X[f * nk + k] for f in range(5)]
+        m = X[5 * nk + k]
+        new, running = substep(q, m, levg[...], run[...], cors[...])
+        run[...] = running
+        new = [jnp.where(copy_row, a[0:1, :], a) for a in new]
+        for f in range(5):
+            X[f * nk + k] = new[f]
+        lev2s[0] += ALPHA * new[2] - BETA * new[3]
+        lev2s[1] += m * pen[k]
+        return c
+
+    lax.fori_loop(0, nk, level, 0)
+
+    @pl.when(lev == 0)
+    def _():
+        to_lower2.start()
+        lev2g[...] = jnp.zeros((2, EXT, WX), F32)
+
     FX[:, pl.ds(0, ROWS), pl.ds(pl.multiple_of(lev * HW, HW), HW)] = half[...]
     to_partner.wait_recv()
     FX[:, pl.ds(0, ROWS), pl.ds(pl.multiple_of(other * HW, HW), HW)] = partner[...]
@@ -451,7 +556,7 @@
         )
         for i in range(2):
             take(foldgot.at[0, pl.ds(0, nlon - 1)], fr.at[i])
-        b1 = (hinge[0] // W + nlon - lon) % nlon
+        b1 = (block + nlon - lon) % nlon
         b0 = (b1 + nlon - 1) % nlon
         outs = [jnp.zeros((24, W), F32), jnp.zeros((24, W), F32)]
         for i, b in enumerate((b0, b1)):
@@ -460,7 +565,7 @@
                 for q in range(2):
                     at = i * W + h * HW + q * 128
                     keep = jnp.where(iota((24, 128), 0) % 2 == q, tile.astype(F32), 0.0).astype(BF16)
-                    outs[q] += jnp.dot(keep, mirror[pl.ds(at, 128), :], preferred_element_type=F32)
+                    outs[q] += jnp.dot(keep, mirror[pl.ds(at, 128), pl.ds(0, W)], preferred_element_type=F32)
         sums = [o[0:8] + o[8:16] + o[16:24] for o in outs]
         for c in range(3):
             rowsgot2(FX, c, sums[0][2 * c : 2 * c + 1] + sums[1][2 * c + 1 : 2 * c + 2], first, W)
@@ -495,7 +600,10 @@
     take(metas.at[pl.ds(0, NP - 1)], ms)
     for c in range(3):
         take(pk.at[c, pl.ds(0, NP - 1)], ss.at[c])
-        take(dense.at[c, pl.ds(0, nz - 1)], zs.at[c])
+        for s in range(ahead):
+            hop(c, s, True).wait_send()
+        for s in range(behind):
+            hop(c, s, False).wait_send()
     to_west.wait_send()
     to_east.wait_send()
     to_partner.wait_send()
@@ -522,6 +630,15 @@
     @pl.when(top)
     def _():
         take(foldgot.at[:, pl.ds(0, nlon - 1)], fs)
+        for a in range(4):
+
+            @pl.when(there[a] != lon)
+            def _():
+                first_hop[a].wait_send()
+
+        for a in second_hop:
+            a.wait_send()
+        third_hop.wait_send()
 
 
 def ps2(ref, i):
@@ -564,24 +681,9 @@
     tiles = flux_tiles.shape[0]
     nz, NP = nlon // 2, 2 * nlat
     N, HW, WX, nfk = NP * 2 * nz, W // 2, W + 128, 6 * nk
-    hinge = fold_partner[0:1]
-
-    with jax.named_scope("fold_rows"):
-        signs = jnp.array([-1.0, -1.0, 1.0, 1.0, 1.0], F32)[:, None, None, None]
-        pair = jnp.concatenate([state[:, :, rows - 1 :], state[:, :, rows - 2 : rows - 1]], axis=2) * signs
-        wet = mask[:, rows - 1 :].astype(F32)
-        wet = jnp.concatenate([wet, jnp.full_like(wet, coriolis[rows - 1])], axis=1)
-        pair = jnp.concatenate([pair, wet[None]], axis=0).reshape(2 * nfk, W)
-
-        def turned(block, value):
-            at = lambda i: i * nlat + nlat - 1
-            high = [(at(i), at((block - i) % nlon)) for i in range(nlon)]
-            low = [(at(i), at((block - 1 - i) % nlon)) for i in range(nlon)]
-            return lax.ppermute(value, ("lon", "lat"), low), lax.ppermute(value, ("lon", "lat"), high)
-
-        fold_lo, fold_hi = lax.switch(hinge[0] // W, [functools.partial(turned, b) for b in range(nlon)], pair)
-
-    vmem, smem, hbm = (pl.BlockSpec(memory_space=s) for s in (pltpu.VMEM, pltpu.SMEM, pl.ANY))
+
+    up, down = nz // 2, max(1, nz - 1 - nz // 2)
+    vmem, smem, hbm = (pl.BlockSpec(memory_space=s) for s in (pltpu.VMEM, pltpu.SMEM, pltpu.HBM))
     V = lambda *s: pltpu.VMEM(s, F32)
     D = lambda *s: pltpu.SemaphoreType.DMA(s)
     X, FX, PX = pl.pallas_call(
@@ -591,26 +693,30 @@
             jax.ShapeDtypeStruct((3, EXT, WX), F32),
             jax.ShapeDtypeStruct((2, EXT, WX), F32),
         ),
-        in_specs=[hbm, hbm, smem, smem, hbm, vmem, vmem, smem, vmem, vmem],
+        in_specs=[hbm] * 8,
         out_specs=(vmem, vmem, vmem),
         scratch_shapes=[
             V(3, tiles, HW), pltpu.VMEM((nk, ROWS, W), I32),
             V(3, NP, 2 * nz, HW), V(3, NP, 2 * nz, HW), V(8, 128), V(NP, 8, 128),
-            V(3, nz, ROWS, HW), V(3, nz, ROWS, HW), V(3, ROWS, HW), V(3, ROWS, HW),
+            V(3, nz, ROWS, HW), V(3, up, ROWS, HW), V(3, up, ROWS, HW), V(3, down, ROWS, HW), V(3, down, ROWS, HW),
+            V(3, ROWS, HW), V(3, ROWS, HW),
             V(2, 8, 128), V(2, 2, 8, 128), V(2, 3, ROWS, 128), V(2, nlon, 8, 128),
-            V(2, nfk // 4, 8, W), V(2, nfk // 4, 8, W), V(2, EXT, 128), V(2, EXT, 128),
-            V(EXT, WX), V(EXT, WX), V(2, EXT, WX), V(2, EXT, WX), V(EXT, WX), pltpu.VMEM((2 * W, W), BF16),
-            D(3), pltpu.SemaphoreType.DMA, pltpu.SemaphoreType.DMA, D(3), D(3), D(3), D(3), D(2), D(2), D(2), D(2),
+            V(2, nfk // 4, 8, W), V(2, nfk // 4, 8, W),
+            V(nfk // 4, 8, W), V(4, nfk // 4, 8, W), V(nfk // 4, 8, W), V(6, nfk // 4, 8, W), V(nfk // 4, 8, WX), pltpu.SMEM((1024,), I32),
+            pltpu.SMEM((ROWS,), F32), pltpu.SMEM((nk,), F32), pltpu.VMEM((1, tiles), I32), pltpu.VMEM((1, tiles), I32),
+            V(2, EXT, 128), V(2, EXT, 128),
+            V(EXT, WX), V(EXT, WX), V(2, EXT, WX), V(2, EXT, WX), V(EXT, WX), pltpu.VMEM((2 * W + 128, WX), BF16),
+            D(8), pltpu.SemaphoreType.DMA, pltpu.SemaphoreType.DMA, D(3), D(3), D(3, up), D(3, up), D(3, down), D(3, down), D(2), D(2), D(2), D(2),
             pltpu.SemaphoreType.DMA, pltpu.SemaphoreType.DMA, pltpu.SemaphoreType.DMA, pltpu.SemaphoreType.DMA,
-            D(5), D(5), D(2), D(2), pltpu.SemaphoreType.DMA, D(2),
+            D(5), D(5), D(2), D(2), pltpu.SemaphoreType.DMA, D(2), D(4), D(4), D(5), D(5),
         ],
         compiler_params=pltpu.CompilerParams(
-            collective_id=0, has_side_effects=True, vmem_limit_bytes=40 * 1024 * 1024
+            collective_id=0, has_side_effects=True, vmem_limit_bytes=60 * 1024 * 1024
         ),
         name="exchange",
     )(
         state.reshape(5 * nk, rows, W), mask, coriolis, penetration, flux_tiles.transpose(1, 0, 2),
-        flux_owner.reshape(1, tiles), flux_row.reshape(1, tiles), hinge, fold_lo, fold_hi,
+        flux_owner.reshape(1, tiles), flux_row.reshape(1, tiles), fold_partner,
     )
 
     return pl.pallas_call(

time: 69.7 us -> 54.3 us (0.78)
  the two profiles are of different devices: /device:TPU:1 before, /device:TPU:4 now
where the time goes in v2:
time: 54.3 us; the launch traced here: 53.8 us
  Pallas kernels  50.1 us (92%)
  local copies, waits for them, and re-layouts  3.66 us (7%)
    pallas_call x1, Pallas kernels, body(): pl.pallas_call(functools.partial(exchange_kernel, nlon, nlat, tiles, nk,...  45.5 us
    pallas_call x1, Pallas kernels, body(): pl.pallas_call(functools.partial(finish_kernel, nk, W), grid=(nk,), out_s...  4.57 us
    unnamed x10, local copies, waits for them, and re-layouts  3.66 us

profile of v2, /device:TPU:4, one launch (start us, length us, event | category | flops | bytes accessed | tf_op | source)
XLA Modules:
  0.0 53.8 jit_solution(13230369897531431246)
XLA Ops:
  0.0 0.0 copy-start.4
  0.0 0.0 copy-start.3
  0.0 45.5 %exchange.1 = (f32[48,24,640]{2,1,0:T(8,128)}, f32[3,24,640]{2,1,0:T(8,128)}, f32[2,24,640]{2,1,0:T(8,128)}) custom-call(f32[40,16,512]{2,1,0:T(8,128)} %bitcast.6, s32[8,16,512]{2,1,0:T(8,128)} %mask.1, f32[16]{0:T(128)} %cor.1, f32[8]{0:T(128)} %pen.1, f32[3,128,512]{2,1,0:T(8,128)} %bitcast.7, s32[1,128]{1,0:T(1,128)} %bitcast.8, s32[1,128]{1,0:T(1,128)} %bitcast.9, ...), custom_call_target="tpu_custom_call" | custom-call | tf_op jit(solution)/shard_map/exchange/pallas_call | solution.py:689
  45.5 0.0 copy-done.4
  45.6 0.0 copy-done.3
  45.6 0.0 copy-start
  45.6 1.8 %copy-done = f32[48,24,640]{2,1,0:T(8,128)S(1)} copy-done((f32[48,24,640]{2,1,0:T(8,128)S(1)}, f32[48,24,640]{2,1,0:T(8,128)}, u32[]{:S(2)}) %copy-start) | copy-done | bytes 2949144
  47.4 0.0 copy-start.1
  47.4 0.9 %copy-done.1 = f32[3,24,640]{2,1,0:T(8,128)S(1)} copy-done((f32[3,24,640]{2,1,0:T(8,128)S(1)}, f32[3,24,640]{2,1,0:T(8,128)}, u32[]{:S(2)}) %copy-start.1) | copy-done | bytes 184344
  48.3 0.0 copy-start.2
  48.3 0.9 %copy-done.2 = f32[2,24,640]{2,1,0:T(8,128)S(1)} copy-done((f32[2,24,640]{2,1,0:T(8,128)S(1)}, f32[2,24,640]{2,1,0:T(8,128)}, u32[]{:S(2)}) %copy-start.2) | copy-done | bytes 122904
  49.2 4.6 %finish.1 = f32[5,8,16,512]{3,2,1,0:T(8,128)} custom-call(f32[6,8,24,640]{3,2,1,0:T(8,128)S(1)} %bitcast.5, f32[3,24,640]{2,1,0:T(8,128)S(1)} %copy-done.1, f32[2,24,640]{2,1,0:T(8,128)S(1)} %copy-done.2, f32[16]{0:T(128)S(1)} %copy-done.3, f32[8]{0:T(128)S(1)} %copy-done.4), custom_call_target="tpu_custom_call" | custom-call | tf_op jit(solution)/shard_map/finish/pallas_call | solution.py:722
Async XLA Ops:
  0.0 45.5 %copy-start.4 = (f32[8]{0:T(128)S(1)}, f32[8]{0:T(128)}, u32[]{:S(2)}) copy-start(f32[8]{0:T(128)} %pen.1) | copy-start | bytes 100
  0.0 45.6 %copy-start.3 = (f32[16]{0:T(128)S(1)}, f32[16]{0:T(128)}, u32[]{:S(2)}) copy-start(f32[16]{0:T(128)} %cor.1) | copy-start | bytes 196
  45.6 1.8 %copy-start = (f32[48,24,640]{2,1,0:T(8,128)S(1)}, f32[48,24,640]{2,1,0:T(8,128)}, u32[]{:S(2)}) copy-start(f32[48,24,640]{2,1,0:T(8,128)} %get-tuple-element.8) | copy-start | bytes 8847364
  47.4 0.9 %copy-start.1 = (f32[3,24,640]{2,1,0:T(8,128)S(1)}, f32[3,24,640]{2,1,0:T(8,128)}, u32[]{:S(2)}) copy-start(f32[3,24,640]{2,1,0:T(8,128)} %get-tuple-element.9.FX) | copy-start | bytes 552964
  48.3 0.9 %copy-start.2 = (f32[2,24,640]{2,1,0:T(8,128)S(1)}, f32[2,24,640]{2,1,0:T(8,128)}, u32[]{:S(2)}) copy-start(f32[2,24,640]{2,1,0:T(8,128)} %get-tuple-element.10.PX) | copy-start | bytes 368644

commit v3 on v2

--- a/solution.py
+++ b/solution.py
@@ -57,10 +57,10 @@
 def exchange_kernel(
     nlon, nlat, tiles, nk, W,
     state, mask, cor_hbm, pen_hbm, flux, owner_hbm, row_hbm, columns_ref,
-    X, FX, PX,
-    tbuf, mbuf, pk, got, meta, metas, dense, east_out, east_in, west_out, west_in, half, partner, frow, rowsgot, colsgot, foldgot,
+    result,
+    X, FX, tail, outs, tbuf, mbuf, pk, got, meta, metas, dense, east_out, east_in, west_out, west_in, half, partner, frow, rowsgot, colsgot, foldgot,
     hsend, hgot, fold, folda, foldm, foldb, fold_rows, hinge, cor, pen, owner_ref, row_ref, esend, egot, levs, levg, lev2s, lev2g, cors, mirror,
-    ld, ms, mr, ss, sr, zes, zer, zws, zwr, hs, hr, es, er, ls, lr, ps, pr, rs, rr, cs, cr, fs, fr, gas, gar, gbs, gbr,
+    ld, ms, mr, ss, sr, zes, zer, zws, zwr, hs, hr, es, er, ls, lr, ps, pr, rs, rr, cs, cr, fs, fr, gas, gar, gbs, gbr, ds,
 ):
     lon, lat, lev = lax.axis_index("lon"), lax.axis_index("lat"), lax.axis_index("lev")
     nz, NP = nlon // 2, 2 * nlat
@@ -158,7 +158,8 @@
         pk[c] = out.reshape(NP, 2 * nz, HW)
 
     load_t.wait()
-    pack(0)
+    for c in range(3):
+        pack(c)
 
     load_s.wait()
     load_m.wait()
@@ -205,37 +206,10 @@
         foldm.at[:, :, edge_of], foldb.at[5, :, :, edge_of], gbs.at[4], gbr.at[4], {"lon": (lon + 3) % nlon}
     )
 
-    @pl.when(top)
-    def _():
-        for a in range(4):
-
-            @pl.when(there[a] != lon)
-            def _():
-                first_hop[a].start()
-
-            @pl.when(there[a] == lon)
-            def _():
-                folda[a] = fold[...]
-
-    to_south = remote(hsend.at[0], hgot.at[0], hs.at[0], hr.at[0], {"lat": jnp.maximum(lat - 1, 0)})
-    to_north = remote(hsend.at[1], hgot.at[1], hs.at[1], hr.at[1], {"lat": jnp.minimum(lat + 1, nlat - 1)})
-
-    @pl.when(jnp.logical_not(bottom))
-    def _():
-        to_south.start()
-
-    @pl.when(jnp.logical_not(top))
-    def _():
-        to_north.start()
-
-
-    def send_meta(d, c):
+    def send_plane(d, c):
         p = (me + d) % NP
         remote(meta, metas.at[me], ms, mr, plane(p)).start()
         return c
-
-    lax.fori_loop(1, NP, send_meta, 0)
-    metas[me] = meta[...]
 
     def send_blocks(c):
         def one(d, carry):
@@ -246,10 +220,34 @@
         lax.fori_loop(1, NP, one, 0)
         got[c, me] = pk[c, me]
 
+    lax.fori_loop(1, NP, send_plane, 0)
+    metas[me] = meta[...]
     send_blocks(0)
-    for c in (1, 2):
-        pack(c)
-        send_blocks(c)
+    @pl.when(top)
+    def _():
+        for a in range(4):
+
+            @pl.when(there[a] != lon)
+            def _():
+                first_hop[a].start()
+
+            @pl.when(there[a] == lon)
+            def _():
+                folda[a] = fold[...]
+
+    send_blocks(1)
+    send_blocks(2)
+    to_south = remote(hsend.at[0], hgot.at[0], hs.at[0], hr.at[0], {"lat": jnp.maximum(lat - 1, 0)})
+    to_north = remote(hsend.at[1], hgot.at[1], hs.at[1], hr.at[1], {"lat": jnp.minimum(lat + 1, nlat - 1)})
+
+    @pl.when(jnp.logical_not(bottom))
+    def _():
+        to_south.start()
+
+    @pl.when(jnp.logical_not(top))
+    def _():
+        to_north.start()
+
 
     load_h.wait()
     block, shifted = hinge[0] // W, hinge[0] % W
@@ -319,6 +317,27 @@
 
         ring(c, 0)
 
+    for c in range(3):
+        landed(c)
+
+    @pl.when(top)
+    def _():
+        for a in range(4):
+
+            @pl.when(there[a] != lon)
+            def _():
+                first_hop[a].wait_recv()
+
+        def pick(g, c):
+            foldm[g] = folda[digit % 4, g]
+            foldb[2, g] = folda[digit % 4, g]
+            return c
+
+        lax.fori_loop(0, nfk // 4, pick, 0)
+        for a in second_hop:
+            a.start()
+        third_hop.start()
+
     @pl.when(jnp.logical_not(top))
     def _():
         to_south.wait_recv()
@@ -360,7 +379,8 @@
     to_east.start()
 
     for c in range(3):
-        landed(c)
+        ring(c, 1)
+
     to_west.wait_recv()
     to_east.wait_recv()
     fe, fw = egot[0], egot[1]
@@ -375,26 +395,21 @@
 
     lax.fori_loop(0, 6, cols_in, 0)
 
-    for c in range(3):
-        ring(c, 1)
-
-    @pl.when(top)
-    def _():
-        for a in range(4):
-
-            @pl.when(there[a] != lon)
-            def _():
-                first_hop[a].wait_recv()
-
-        def pick(g, c):
-            foldm[g] = folda[digit % 4, g]
-            foldb[2, g] = folda[digit % 4, g]
+    to_lower = remote(levs, levg, ls, lr, {"lev": 1})
+    to_lower2 = remote(lev2s, lev2g, ps, pr, {"lev": 1})
+
+    def shallower():
+        levs[...] = ALPHA * X[2 * nk] - BETA * X[3 * nk]
+
+        def add(k, c):
+            levs[...] += ALPHA * X[2 * nk + k] - BETA * X[3 * nk + k]
             return c
 
-        lax.fori_loop(0, nfk // 4, pick, 0)
-        for a in second_hop:
-            a.start()
-        third_hop.start()
+        lax.fori_loop(1, nk, add, 0)
+        to_lower.start()
+        levg[...] = jnp.zeros((EXT, WX), F32)
+
+    pl.when((lev == 0) & jnp.logical_not(top))(shallower)
 
     for s in range(2, ahead):
         for c in range(3):
@@ -473,20 +488,7 @@
 
         lax.fori_loop(0, nfk // 4, insert, 0)
 
-    to_lower = remote(levs, levg, ls, lr, {"lev": 1})
-    to_lower2 = remote(lev2s, lev2g, ps, pr, {"lev": 1})
-
-    @pl.when(lev == 0)
-    def _():
-        levs[...] = ALPHA * X[2 * nk] - BETA * X[3 * nk]
-
-        def add(k, c):
-            levs[...] += ALPHA * X[2 * nk + k] - BETA * X[3 * nk + k]
-            return c
-
-        lax.fori_loop(1, nk, add, 0)
-        to_lower.start()
-        levg[...] = jnp.zeros((EXT, WX), F32)
+    pl.when((lev == 0) & top)(shallower)
 
     row_id = iota((EXT, WX), 0)
     turning = jnp.where(row_id == ROWS, X[5 * nk, pl.ds(17, 1), :], X[5 * nk, pl.ds(22, 1), :])
@@ -499,7 +501,7 @@
         to_lower.wait_recv()
 
     lev2s[...] = jnp.zeros((2, EXT, WX), F32)
-    run = PX.at[0]
+    run = tail.at[0]
     run[...] = jnp.zeros((EXT, WX), F32)
     copy_row = (row_id == EXT - 1) & bottom
 
@@ -595,11 +597,40 @@
     def _():
         to_lower2.wait_recv()
 
-    PX[...] = lev2g[...]
+    extra = ALPHA * FX[0] - BETA * FX[1]
+    tail[1] = lev2g[0] + lev2g[1] * extra
+    tail[0] = jnp.zeros((EXT, WX), F32)
+
+    def store(k):
+        return pltpu.make_async_copy(outs.at[k % 2], result.at[:, k], ds.at[k % 2])
+
+    def finish(k, c):
+        m = X[5 * nk + k]
+        gain = m * pen[k]
+        push = [gain * FX[i] for i in range(3)]
+        q = [X[f * nk + k] + push[f - 2] if f > 1 else X[f * nk + k] for f in range(5)]
+        new, running = substep(q, m, tail[1], tail[0], cors[...])
+        tail[0] = running
+
+        @pl.when(k >= 2)
+        def _():
+            store(k - 2).wait()
+
+        for f in range(5):
+            value = new[f] + push[f - 2] if f > 1 else new[f]
+            outs[k % 2, f] = value[0:ROWS, 0:W]
+        store(k).start()
+        return c
+
+    lax.fori_loop(0, nk, finish, 0)
+
+    store(nk - 2).wait()
+    store(nk - 1).wait()
 
     take(metas.at[pl.ds(0, NP - 1)], ms)
     for c in range(3):
         take(pk.at[c, pl.ds(0, NP - 1)], ss.at[c])
+    for c in range(3):
         for s in range(ahead):
             hop(c, s, True).wait_send()
         for s in range(behind):
@@ -649,32 +680,6 @@
     FX[c, pl.ds(ROWS, 8), pl.ds(0, W)] = jnp.where(first, line, 0.0)
 
 
-def finish_kernel(nk, W, X, FX, PX, cor, pen, out, run):
-    k = pl.program_id(0)
-    WX = W + 128
-    row_id = iota((EXT, WX), 0)
-
-    @pl.when(k == 0)
-    def _():
-        run[0] = jnp.zeros((EXT, WX), F32)
-        extra = ALPHA * FX[0] - BETA * FX[1]
-        run[1] = PX[0] + PX[1] * extra
-        turning = jnp.zeros((EXT, WX), F32)
-        for i in range(ROWS):
-            turning = jnp.where(row_id == i, cor[i], turning)
-        run[2] = turning
-
-    m = X[5, 0]
-    gain = m * pen[k]
-    push = [gain * FX[c] for c in range(3)]
-    q = [X[f, 0] + push[f - 2] if f > 1 else X[f, 0] for f in range(5)]
-    new, running = substep(q, m, run[1], run[0], run[2])
-    run[0] = running
-    for f in range(5):
-        result = new[f] + push[f - 2] if f > 1 else new[f]
-        out[f, 0] = result[0:ROWS, 0:W]
-
-
 def body(state, mask, coriolis, penetration, flux_tiles, flux_owner, flux_row, fold_partner):
     _, nk, rows, W = state.shape
     nlon, nlat = lax.axis_size("lon"), lax.axis_size("lat")
@@ -683,19 +688,16 @@
     N, HW, WX, nfk = NP * 2 * nz, W // 2, W + 128, 6 * nk
 
     up, down = nz // 2, max(1, nz - 1 - nz // 2)
-    vmem, smem, hbm = (pl.BlockSpec(memory_space=s) for s in (pltpu.VMEM, pltpu.SMEM, pltpu.HBM))
+    hbm = pl.BlockSpec(memory_space=pl.ANY)
     V = lambda *s: pltpu.VMEM(s, F32)
     D = lambda *s: pltpu.SemaphoreType.DMA(s)
-    X, FX, PX = pl.pallas_call(
+    return pl.pallas_call(
         functools.partial(exchange_kernel, nlon, nlat, tiles, nk, W),
-        out_shape=(
-            jax.ShapeDtypeStruct((nfk, EXT, WX), F32),
-            jax.ShapeDtypeStruct((3, EXT, WX), F32),
-            jax.ShapeDtypeStruct((2, EXT, WX), F32),
-        ),
+        out_shape=jax.ShapeDtypeStruct(state.shape, F32),
         in_specs=[hbm] * 8,
-        out_specs=(vmem, vmem, vmem),
+        out_specs=hbm,
         scratch_shapes=[
+            V(nfk, EXT, WX), V(3, EXT, WX), V(2, EXT, WX), V(2, 5, ROWS, W),
             V(3, tiles, HW), pltpu.VMEM((nk, ROWS, W), I32),
             V(3, NP, 2 * nz, HW), V(3, NP, 2 * nz, HW), V(8, 128), V(NP, 8, 128),
             V(3, nz, ROWS, HW), V(3, up, ROWS, HW), V(3, up, ROWS, HW), V(3, down, ROWS, HW), V(3, down, ROWS, HW),
@@ -708,7 +710,7 @@
             V(EXT, WX), V(EXT, WX), V(2, EXT, WX), V(2, EXT, WX), V(EXT, WX), pltpu.VMEM((2 * W + 128, WX), BF16),
             D(8), pltpu.SemaphoreType.DMA, pltpu.SemaphoreType.DMA, D(3), D(3), D(3, up), D(3, up), D(3, down), D(3, down), D(2), D(2), D(2), D(2),
             pltpu.SemaphoreType.DMA, pltpu.SemaphoreType.DMA, pltpu.SemaphoreType.DMA, pltpu.SemaphoreType.DMA,
-            D(5), D(5), D(2), D(2), pltpu.SemaphoreType.DMA, D(2), D(4), D(4), D(5), D(5),
+            D(5), D(5), D(2), D(2), pltpu.SemaphoreType.DMA, D(2), D(4), D(4), D(5), D(5), D(2),
         ],
         compiler_params=pltpu.CompilerParams(
             collective_id=0, has_side_effects=True, vmem_limit_bytes=60 * 1024 * 1024
@@ -718,23 +720,6 @@
         state.reshape(5 * nk, rows, W), mask, coriolis, penetration, flux_tiles.transpose(1, 0, 2),
         flux_owner.reshape(1, tiles), flux_row.reshape(1, tiles), fold_partner,
     )
-
-    return pl.pallas_call(
-        functools.partial(finish_kernel, nk, W),
-        grid=(nk,),
-        out_shape=jax.ShapeDtypeStruct(state.shape, F32),
-        in_specs=[
-            pl.BlockSpec((6, 1, EXT, WX), lambda k: (0, k, 0, 0)),
-            pl.BlockSpec((3, EXT, WX), lambda k: (0, 0, 0)),
-            pl.BlockSpec((2, EXT, WX), lambda k: (0, 0, 0)),
-            smem,
-            smem,
-        ],
-        out_specs=pl.BlockSpec((5, 1, rows, W), lambda k: (0, k, 0, 0)),
-        scratch_shapes=[V(3, EXT, WX)],
-        compiler_params=pltpu.CompilerParams(vmem_limit_bytes=32 * 1024 * 1024),
-        name="finish",
-    )(X.reshape(6, nk, EXT, WX), FX, PX, coriolis, penetration)
 
 
 def solution(mesh):

time: 54.3 us -> 51.3 us (0.945)
  the two profiles are of different devices: /device:TPU:4 before, /device:TPU:29 now
where the time goes in v3:
time: 51.3 us; the launch traced here: 51.2 us
  Pallas kernels  48.6 us (95%)
  local copies, waits for them, and re-layouts  2.54 us (5%)
    pallas_call x1, Pallas kernels, body(): pl.pallas_call(functools.partial(exchange_kernel, nlon, nlat, tiles, nk,...  48.6 us
    unnamed x1, local copies, waits for them, and re-layouts  2.54 us

profile of v3, /device:TPU:29, one launch (start us, length us, event | category | flops | bytes accessed | tf_op | source)
XLA Modules:
  0.0 51.2 jit_solution(688916881243207167)
XLA Ops:
  0.0 48.6 %exchange.1 = f32[5,8,16,512]{3,2,1,0:T(8,128)} custom-call(f32[40,16,512]{2,1,0:T(8,128)} %bitcast.4, s32[8,16,512]{2,1,0:T(8,128)} %mask.1, f32[16]{0:T(128)} %cor_hbm.1, f32[8]{0:T(128)} %pen_hbm.1, f32[3,128,512]{2,1,0:T(8,128)} %bitcast.5, s32[1,128]{1,0:T(1,128)} %bitcast.6, s32[1,128]{1,0:T(1,128)} %bitcast.7, s32[8192]{0:T(1024)} %columns_ref.1), custom_call_target="tpu_custom_call" | custom-call | tf_op jit(solution)/shard_map/exchange/pallas_call | solution.py:694
  48.6 2.5 %copy.10 = f32[5,8,16,512]{3,2,1,0:T(8,128)} copy(f32[5,8,16,512]{3,2,1,0:T(8,128)} %exchange.1) | data formatting | bytes 2621440
